TPU v7x, 32 devices: a whole 2x2x4 slice. The times are simulated.
32 devices in a mesh: seq: 8 (over z, x), seg: 4 (over y, core).
Axes of the slice: x: 2, y: 2, z: 4, core: 2. Of those that a mesh axis runs over, the one named last changes fastest.
Arguments:
- tokens: bfloat16 [4, 2048, 1024], P('seg', 'seq'), may hold values from -6 to 6
- starts: int32 [4, 4], P('seg'), may hold values from 0 to 2047, as said below
- norm_gain: bfloat16 [1024], P(('seq', 'seg')), may hold values from 0.099609375 to 1.8984375
- ema_delta: bfloat16 [1024, 16], P(('seq', 'seg'))
- ema_alpha: bfloat16 [1024, 16], P(('seq', 'seg'))
- ema_beta: bfloat16 [1024, 16], P(('seq', 'seg')), may hold values from -4 to 4
- ema_eta: bfloat16 [1024, 16], P(('seq', 'seg')), may hold values from -1 to 1
- ema_omega: bfloat16 [1024], P(('seq', 'seg')), may hold values from -4 to 4
- mix_weight: bfloat16 [1024, 4224], P('seq', 'seg'), may hold values from -0.1875 to 0.1875
- value_weight: bfloat16 [1024, 2048], P('seq', 'seg'), may hold values from -0.1875 to 0.1875
- qk_affine: bfloat16 [512], P(('seq', 'seg')), may hold values from -4 to 4
- out_weight: bfloat16 [2048, 1024], P('seq', 'seg'), may hold values from -0.25 to 0.25
- ffn_gain: bfloat16 [1024], P(('seq', 'seg')), may hold values from 0.099609375 to 1.8984375
- ffn_in: bfloat16 [1024, 4096], P('seq', 'seg'), may hold values from -0.1875 to 0.1875
- ffn_out: bfloat16 [4096, 1024], P('seq', 'seg'), may hold values from -0.09375 to 0.09375
- cotangent: bfloat16 [4, 2048, 1024], P('seg', 'seq'), may hold values from -6 to 6
Outputs:
- layer_out: bfloat16 [4, 2048, 1024], P('seg', 'seq')
- grad_tokens: bfloat16 [4, 2048, 1024], P('seg', 'seq')
- grad_norm_gain: float32 [1024], P(('seq', 'seg'))
- grad_ema_delta: float32 [1024, 16], P(('seq', 'seg'))
- grad_ema_alpha: float32 [1024, 16], P(('seq', 'seg'))
- grad_ema_beta: float32 [1024, 16], P(('seq', 'seg'))
- grad_ema_eta: float32 [1024, 16], P(('seq', 'seg'))
- grad_ema_omega: float32 [1024], P(('seq', 'seg'))
- grad_mix_weight: float32 [1024, 4224], P('seq', 'seg')
- grad_value_weight: float32 [1024, 2048], P('seq', 'seg')
- grad_qk_affine: float32 [512], P(('seq', 'seg'))
- grad_out_weight: float32 [2048, 1024], P('seq', 'seg')
- grad_ffn_gain: float32 [1024], P(('seq', 'seg'))
- grad_ffn_in: float32 [1024, 4096], P('seq', 'seg')
- grad_ffn_out: float32 [4096, 1024], P('seq', 'seg')
Inputs may be any that keep to these rules, and one draw needn't show every extreme that they name: Each row begins with 0 and never falls; document k of a segment runs from starts[k] to the next entry, the last one to the end of the segment.
All inputs are finite; a program needn't handle non-finite values.
Results may differ from a plain program's by a relative error of at most 0.02.
Values may be sent and summed in bfloat16 or wider, within the bound.
A program may use at most 512 MiB of HBM per device.

v0:
```python
import jax
import jax.numpy as jnp
from jax import lax
from jax.sharding import PartitionSpec as P

STRETCH = 128


epsilon = 1e-05
highest = lax.Precision.HIGHEST


def ema_apply(
    inputs, documents, damp_logit, decay_logit, inflow_gain, outflow_gain, omega_gain, block_len
):
    seg_count, length, channels = inputs.shape
    damping = jax.nn.sigmoid(damp_logit)
    log_keep = jnp.log1p(-damping * jax.nn.sigmoid(decay_logit))
    inflow = damping * inflow_gain
    offsets = jnp.arange(block_len)
    steps_f = offsets.astype(inputs.dtype)
    powers = jnp.exp(steps_f[:, None, None] * log_keep[None])
    kernel = jnp.sum(powers * (inflow * outflow_gain)[None], axis=2)
    carry_out = jnp.exp((steps_f + 1.0)[:, None, None] * log_keep[None]) * outflow_gain[None]
    feed_pow = jnp.exp((block_len - 1.0 - steps_f)[:, None, None] * log_keep[None]) * inflow[None]
    full_keep = jnp.exp(block_len * log_keep)
    lag_steps = offsets[:, None] - offsets[None, :]
    lower_tri = lag_steps >= 0
    selector = (jnp.maximum(lag_steps, 0)[:, :, None] == offsets[None, None, :]).astype(
        inputs.dtype
    )
    toeplitz = jnp.dot(
        selector.reshape(block_len * block_len, block_len), kernel, precision=highest
    ).reshape(block_len, block_len, channels)
    blocks = length // block_len
    pieces = inputs.reshape(seg_count, blocks, block_len, channels).transpose(1, 0, 2, 3)
    labels = documents.reshape(seg_count, blocks, block_len).transpose(1, 0, 2)
    before = jnp.concatenate([jnp.zeros((1, seg_count), jnp.int32), labels[:-1, :, -1]], axis=0)

    def advance(carry_state, block_item):
        values, block_docs, earlier = block_item
        same_doc = ((block_docs[:, :, None] == block_docs[:, None, :]) & lower_tri[None]).astype(
            values.dtype
        )
        inside = jnp.einsum("isc,nis,nsc->nic", toeplitz, same_doc, values, precision=highest)
        alive_rows = (block_docs == earlier[:, None]).astype(values.dtype)
        carried = alive_rows[:, :, None] * jnp.einsum(
            "ich,nch->nic", carry_out, carry_state, precision=highest
        )
        tail_mask = (block_docs == block_docs[:, -1:]).astype(values.dtype)
        fresh_state = jnp.einsum("ns,nsc,sch->nch", tail_mask, values, feed_pow, precision=highest)
        next_state = alive_rows[:, -1][:, None, None] * full_keep[None] * carry_state + fresh_state
        return (next_state, inside + carried)

    start_state = jnp.zeros((seg_count, channels, log_keep.shape[1]), inputs.dtype)
    _, outputs = lax.scan(advance, start_state, (pieces, labels, before))
    return outputs.transpose(1, 0, 2, 3).reshape(seg_count, length, channels) + omega_gain * inputs


def rms_forward(values, gain):
    inverse = lax.rsqrt(jnp.mean(values * values, axis=-1, keepdims=True) + epsilon)
    return (values * inverse * gain, inverse)


def rms_backward(grad_out, values, inverse, gain):
    scaled = grad_out * gain
    projection = jnp.mean(scaled * values, axis=-1, keepdims=True)
    grad_in = inverse * (scaled - values * inverse * inverse * projection)
    return (grad_in, jnp.sum(grad_out * values * inverse, axis=0))


def silu_slope(values):
    sigma_v = jax.nn.sigmoid(values)
    return sigma_v * (1.0 + values * (1.0 - sigma_v))


def over_rows(left, right):
    return lax.dot_general(
        left, right, (((0,), (0,)), ((), ())), preferred_element_type=jnp.float32
    )


def against(left, right):
    return lax.dot_general(
        left, right, (((1,), (1,)), ((), ())), preferred_element_type=jnp.float32
    )


def masked_scores(query_blk, key_blk, allowed):
    raw_scores = jnp.einsum("cid,cjd->cij", query_blk, key_blk, preferred_element_type=jnp.float32)
    return jnp.where(allowed, raw_scores, -1e30)


def widen(local_part, first_row, full_rows):
    holder = jnp.zeros((full_rows,) + local_part.shape[1:], jnp.float32)
    return lax.dynamic_update_slice_in_dim(holder, local_part, first_row, 0)


def body(
    tokens,
    starts,
    norm_gain,
    ema_delta,
    ema_alpha,
    ema_beta,
    ema_eta,
    ema_omega,
    mix_weight,
    value_weight,
    qk_affine,
    out_weight,
    ffn_gain,
    ffn_in,
    ffn_out,
    cotangent,
):
    seg_count, row_count, model_width = tokens.shape
    seq_lanes = lax.axis_size("seq")
    seq_index = lax.axis_index("seq")
    seq_length = row_count * seq_lanes
    chan_count = model_width // seq_lanes
    token_count = seg_count * row_count
    part_set = (
        lax.all_gather(norm_gain[None], "seg", axis=1, tiled=True),
        lax.all_gather(ema_delta[None], "seg", axis=1, tiled=True),
        lax.all_gather(ema_alpha[None], "seg", axis=1, tiled=True),
        lax.all_gather(ema_beta[None], "seg", axis=1, tiled=True),
        lax.all_gather(ema_eta[None], "seg", axis=1, tiled=True),
        lax.all_gather(ema_omega[None], "seg", axis=1, tiled=True),
        lax.all_gather(mix_weight, "seg", axis=1, tiled=True),
        lax.all_gather(value_weight, "seg", axis=1, tiled=True),
        lax.all_gather(qk_affine[None], "seg", axis=1, tiled=True),
        lax.all_gather(out_weight, "seg", axis=1, tiled=True),
        lax.all_gather(ffn_gain[None], "seg", axis=1, tiled=True),
        lax.all_gather(ffn_in, "seg", axis=1, tiled=True),
        lax.all_gather(ffn_out, "seg", axis=1, tiled=True),
    )
    whole_set = (
        lax.all_gather(part_set[0], "seq", axis=0, tiled=True),
        lax.all_gather(part_set[1], "seq", axis=0, tiled=True),
        lax.all_gather(part_set[2], "seq", axis=0, tiled=True),
        lax.all_gather(part_set[3], "seq", axis=0, tiled=True),
        lax.all_gather(part_set[4], "seq", axis=0, tiled=True),
        lax.all_gather(part_set[5], "seq", axis=0, tiled=True),
        lax.all_gather(part_set[6], "seq", axis=0, tiled=True),
        lax.all_gather(part_set[7], "seq", axis=0, tiled=True),
        lax.all_gather(part_set[8], "seq", axis=0, tiled=True),
        lax.all_gather(part_set[9], "seq", axis=0, tiled=True),
        lax.all_gather(part_set[10], "seq", axis=0, tiled=True),
        lax.all_gather(part_set[11], "seq", axis=0, tiled=True),
        lax.all_gather(part_set[12], "seq", axis=0, tiled=True),
    )
    gain_full = whole_set[0].reshape(-1)
    ema_width = whole_set[1].shape[2]
    delta_full = whole_set[1].reshape(-1, ema_width)
    alpha_full = whole_set[2].reshape(-1, ema_width)
    beta_full = whole_set[3].reshape(-1, ema_width)
    eta_full = whole_set[4].reshape(-1, ema_width)
    omega_full = whole_set[5].reshape(-1)
    mix_full = whole_set[6]
    value_full = whole_set[7]
    affine_full = whole_set[8].reshape(-1)
    out_full = whole_set[9]
    ffn_gain_full = whole_set[10].reshape(-1)
    ffn_in_full = whole_set[11]
    ffn_out_full = whole_set[12]
    zdim = affine_full.shape[0] // 4
    vdim = value_full.shape[1]
    tokens_flat = tokens.reshape(token_count, model_width).astype(jnp.float32)
    gain_one = gain_full.astype(jnp.float32)
    normed, inverse_one = rms_forward(tokens_flat, gain_one)
    normed_b = normed.astype(jnp.bfloat16)
    spread = lax.all_to_all(
        normed_b.reshape(seg_count, row_count, model_width),
        "seq",
        split_axis=2,
        concat_axis=1,
        tiled=True,
    )
    chan_start = seq_index * chan_count

    def local_slice(values):
        return lax.dynamic_slice_in_dim(values, chan_start, chan_count, 0).astype(jnp.float32)

    positions_full = jnp.arange(seq_length, dtype=jnp.int32)
    docs_full = jnp.sum(
        (starts[:, None, :] <= positions_full[None, :, None]).astype(jnp.int32), axis=2
    )

    def mixing(inputs, damp_part, decay_part, inflow_part, outflow_part, omega_part):
        return jax.nn.silu(
            ema_apply(
                inputs,
                docs_full,
                damp_part,
                decay_part,
                inflow_part,
                outflow_part,
                omega_part,
                STRETCH,
            )
        )

    mixed_chan, ema_pull = jax.vjp(
        mixing,
        spread.astype(jnp.float32),
        local_slice(delta_full),
        local_slice(alpha_full),
        local_slice(beta_full),
        local_slice(eta_full),
        local_slice(omega_full),
    )
    active = lax.all_to_all(
        mixed_chan.astype(jnp.bfloat16), "seq", split_axis=1, concat_axis=2, tiled=True
    ).reshape(token_count, model_width)
    projected = jnp.dot(active, mix_full, preferred_element_type=jnp.float32)
    update = jax.nn.sigmoid(projected[:, :model_width])
    gate_pre = projected[:, model_width : model_width + zdim + vdim]
    gate_rows = jax.nn.silu(gate_pre)
    shared = gate_rows[:, :zdim]
    reset_gate = gate_rows[:, zdim:]
    candidate = projected[:, model_width + zdim + vdim :]
    value_pre = jnp.dot(normed_b, value_full, preferred_element_type=jnp.float32)
    values_b = jax.nn.silu(value_pre).astype(jnp.bfloat16)
    affine = affine_full.astype(jnp.float32).reshape(4, zdim)
    scale_q = zdim ** (-0.5)
    query_b = (scale_q * (shared * affine[0] + affine[1])).astype(jnp.bfloat16)
    key_b = (shared * affine[2] + affine[3]).astype(jnp.bfloat16)
    positions_rows = seq_index * row_count + jnp.arange(row_count, dtype=jnp.int32)
    docs_rows = jnp.sum(
        (starts[:, None, :] <= positions_rows[None, :, None]).astype(jnp.int32), axis=2
    )
    block_count = token_count // STRETCH
    block_docs = docs_rows.reshape(block_count, STRETCH)
    offsets = jnp.arange(STRETCH)
    allowed = (block_docs[:, :, None] == block_docs[:, None, :]) & (
        offsets[:, None] >= offsets[None, :]
    )[None]
    query_blk = query_b.reshape(block_count, STRETCH, zdim)
    key_blk = key_b.reshape(block_count, STRETCH, zdim)
    value_blk = values_b.reshape(block_count, STRETCH, vdim)
    scores = masked_scores(query_blk, key_blk, allowed)
    row_top = jnp.max(scores, axis=2, keepdims=True)
    expo_scores = jnp.exp(scores - row_top)
    row_total = jnp.sum(expo_scores, axis=2, keepdims=True)
    probs = expo_scores / row_total
    log_total = row_top + jnp.log(row_total)
    attended = jnp.einsum(
        "cij,cjv->civ", probs.astype(jnp.bfloat16), value_blk, preferred_element_type=jnp.float32
    ).reshape(token_count, vdim)
    hidden_in = (attended * reset_gate).astype(jnp.bfloat16)
    hidden_pre = candidate + jnp.dot(hidden_in, out_full, preferred_element_type=jnp.float32)
    hidden_act = jax.nn.silu(hidden_pre)
    out_one = tokens_flat + update * (hidden_act - tokens_flat)
    gain_two = ffn_gain_full.astype(jnp.float32)
    normed_two, inverse_two = rms_forward(out_one, gain_two)
    normed_two_b = normed_two.astype(jnp.bfloat16)
    ffn_hidden = jnp.dot(normed_two_b, ffn_in_full, preferred_element_type=jnp.float32)
    ffn_act = jax.nn.silu(ffn_hidden).astype(jnp.bfloat16)
    result = (out_one + jnp.dot(ffn_act, ffn_out_full, preferred_element_type=jnp.float32)).astype(
        jnp.bfloat16
    )
    grad_y_b = cotangent.reshape(token_count, model_width)
    grad_ffn_out = over_rows(ffn_act, grad_y_b)
    grad_act = against(grad_y_b, ffn_out_full)
    grad_hidden_b = (grad_act * silu_slope(ffn_hidden)).astype(jnp.bfloat16)
    grad_ffn_in = over_rows(normed_two_b, grad_hidden_b)
    grad_normed_two = against(grad_hidden_b, ffn_in_full)
    grad_norm_two, grad_gain_two = rms_backward(grad_normed_two, out_one, inverse_two, gain_two)
    grad_out_one = grad_y_b.astype(jnp.float32) + grad_norm_two
    grad_update = grad_out_one * (hidden_act - tokens_flat)
    grad_tokens_flat = grad_out_one * (1.0 - update)
    grad_hpre_b = (grad_out_one * update * silu_slope(hidden_pre)).astype(jnp.bfloat16)
    grad_out_weight = over_rows(hidden_in, grad_hpre_b)
    grad_hidden_in = against(grad_hpre_b, out_full)
    grad_att_b = (grad_hidden_in * reset_gate).astype(jnp.bfloat16)
    grad_reset = grad_hidden_in * attended
    probs_again = jnp.exp(masked_scores(query_blk, key_blk, allowed) - log_total)
    grad_att_blk = grad_att_b.reshape(block_count, STRETCH, vdim)
    grad_probs = jnp.einsum(
        "civ,cjv->cij", grad_att_blk, value_blk, preferred_element_type=jnp.float32
    )
    weighted = jnp.sum(probs_again * grad_probs, axis=2, keepdims=True)
    grad_scores_b = (probs_again * (grad_probs - weighted)).astype(jnp.bfloat16)
    grad_query = jnp.einsum(
        "cij,cjd->cid", grad_scores_b, key_blk, preferred_element_type=jnp.float32
    ).reshape(token_count, zdim)
    grad_key = jnp.einsum(
        "cij,cid->cjd", grad_scores_b, query_blk, preferred_element_type=jnp.float32
    ).reshape(token_count, zdim)
    grad_values = jnp.einsum(
        "cij,civ->cjv",
        probs_again.astype(jnp.bfloat16),
        grad_att_blk,
        preferred_element_type=jnp.float32,
    ).reshape(token_count, vdim)
    grad_qs = grad_query * scale_q
    grad_shared = grad_qs * affine[0] + grad_key * affine[2]
    grad_affine = jnp.stack(
        [
            jnp.sum(grad_qs * shared, axis=0),
            jnp.sum(grad_qs, axis=0),
            jnp.sum(grad_key * shared, axis=0),
            jnp.sum(grad_key, axis=0),
        ]
    ).reshape(4 * zdim)
    grad_gate_pre = jnp.concatenate([grad_shared, grad_reset], axis=1) * silu_slope(gate_pre)
    grad_upre = grad_update * update * (1.0 - update)
    grad_proj_b = jnp.concatenate(
        [grad_upre, grad_gate_pre, grad_hpre_b.astype(jnp.float32)], axis=1
    ).astype(jnp.bfloat16)
    grad_mix = over_rows(active, grad_proj_b)
    grad_active_b = against(grad_proj_b, mix_full).astype(jnp.bfloat16)
    grad_chan = lax.all_to_all(
        grad_active_b.reshape(seg_count, row_count, model_width),
        "seq",
        split_axis=2,
        concat_axis=1,
        tiled=True,
    )
    grad_ema_in, grad_delta, grad_alpha, grad_beta, grad_eta, grad_omega = ema_pull(
        grad_chan.astype(jnp.float32)
    )
    grad_from_ema = lax.all_to_all(
        grad_ema_in.astype(jnp.bfloat16), "seq", split_axis=1, concat_axis=2, tiled=True
    ).reshape(token_count, model_width)
    grad_vpre_b = (grad_values * silu_slope(value_pre)).astype(jnp.bfloat16)
    grad_value = over_rows(normed_b, grad_vpre_b)
    grad_normed = against(grad_vpre_b, value_full) + grad_from_ema.astype(jnp.float32)
    grad_norm_one, grad_gain_one = rms_backward(grad_normed, tokens_flat, inverse_one, gain_one)
    grad_tokens = (
        (grad_tokens_flat + grad_norm_one)
        .astype(jnp.bfloat16)
        .reshape(seg_count, row_count, model_width)
    )

    def grid_vec(vector):
        return vector.reshape(seq_lanes, -1)

    def grid_tab(table):
        return table.reshape(seq_lanes, -1, table.shape[1])

    terms = (
        grid_vec(grad_gain_one),
        grid_tab(widen(grad_delta, chan_start, model_width)),
        grid_tab(widen(grad_alpha, chan_start, model_width)),
        grid_tab(widen(grad_beta, chan_start, model_width)),
        grid_tab(widen(grad_eta, chan_start, model_width)),
        grid_vec(widen(grad_omega, chan_start, model_width)),
        grad_mix,
        grad_value,
        grid_vec(grad_affine),
        grad_out_weight,
        grid_vec(grad_gain_two),
        grad_ffn_in,
        grad_ffn_out,
    )
    first_sum = (
        lax.psum_scatter(terms[0], "seq", scatter_dimension=0, tiled=True),
        lax.psum_scatter(terms[1], "seq", scatter_dimension=0, tiled=True),
        lax.psum_scatter(terms[2], "seq", scatter_dimension=0, tiled=True),
        lax.psum_scatter(terms[3], "seq", scatter_dimension=0, tiled=True),
        lax.psum_scatter(terms[4], "seq", scatter_dimension=0, tiled=True),
        lax.psum_scatter(terms[5], "seq", scatter_dimension=0, tiled=True),
        lax.psum_scatter(terms[6], "seq", scatter_dimension=0, tiled=True),
        lax.psum_scatter(terms[7], "seq", scatter_dimension=0, tiled=True),
        lax.psum_scatter(terms[8], "seq", scatter_dimension=0, tiled=True),
        lax.psum_scatter(terms[9], "seq", scatter_dimension=0, tiled=True),
        lax.psum_scatter(terms[10], "seq", scatter_dimension=0, tiled=True),
        lax.psum_scatter(terms[11], "seq", scatter_dimension=0, tiled=True),
        lax.psum_scatter(terms[12], "seq", scatter_dimension=0, tiled=True),
    )
    summed = (
        lax.psum_scatter(
            first_sum[0].astype(jnp.bfloat16), "seg", scatter_dimension=1, tiled=True
        ).astype(jnp.float32),
        lax.psum_scatter(
            first_sum[1].astype(jnp.bfloat16), "seg", scatter_dimension=1, tiled=True
        ).astype(jnp.float32),
        lax.psum_scatter(
            first_sum[2].astype(jnp.bfloat16), "seg", scatter_dimension=1, tiled=True
        ).astype(jnp.float32),
        lax.psum_scatter(
            first_sum[3].astype(jnp.bfloat16), "seg", scatter_dimension=1, tiled=True
        ).astype(jnp.float32),
        lax.psum_scatter(
            first_sum[4].astype(jnp.bfloat16), "seg", scatter_dimension=1, tiled=True
        ).astype(jnp.float32),
        lax.psum_scatter(
            first_sum[5].astype(jnp.bfloat16), "seg", scatter_dimension=1, tiled=True
        ).astype(jnp.float32),
        lax.psum_scatter(
            first_sum[6].astype(jnp.bfloat16), "seg", scatter_dimension=1, tiled=True
        ).astype(jnp.float32),
        lax.psum_scatter(
            first_sum[7].astype(jnp.bfloat16), "seg", scatter_dimension=1, tiled=True
        ).astype(jnp.float32),
        lax.psum_scatter(
            first_sum[8].astype(jnp.bfloat16), "seg", scatter_dimension=1, tiled=True
        ).astype(jnp.float32),
        lax.psum_scatter(
            first_sum[9].astype(jnp.bfloat16), "seg", scatter_dimension=1, tiled=True
        ).astype(jnp.float32),
        lax.psum_scatter(
            first_sum[10].astype(jnp.bfloat16), "seg", scatter_dimension=1, tiled=True
        ).astype(jnp.float32),
        lax.psum_scatter(
            first_sum[11].astype(jnp.bfloat16), "seg", scatter_dimension=1, tiled=True
        ).astype(jnp.float32),
        lax.psum_scatter(
            first_sum[12].astype(jnp.bfloat16), "seg", scatter_dimension=1, tiled=True
        ).astype(jnp.float32),
    )
    return (
        result.reshape(seg_count, row_count, model_width),
        grad_tokens,
        summed[0].reshape(-1),
        summed[1].reshape(-1, ema_width),
        summed[2].reshape(-1, ema_width),
        summed[3].reshape(-1, ema_width),
        summed[4].reshape(-1, ema_width),
        summed[5].reshape(-1),
        summed[6],
        summed[7],
        summed[8].reshape(-1),
        summed[9],
        summed[10].reshape(-1),
        summed[11],
        summed[12],
    )


def solution(mesh):
    placed = (
        P("seg", "seq", None),
        P("seg", None),
        P(("seq", "seg")),
        P(("seq", "seg"), None),
        P(("seq", "seg"), None),
        P(("seq", "seg"), None),
        P(("seq", "seg"), None),
        P(("seq", "seg")),
        P("seq", "seg"),
        P("seq", "seg"),
        P(("seq", "seg")),
        P("seq", "seg"),
        P(("seq", "seg")),
        P("seq", "seg"),
        P("seq", "seg"),
        P("seg", "seq", None),
    )
    return jax.shard_map(
        body,
        mesh=mesh,
        in_specs=placed,
        out_specs=(
            P("seg", "seq", None),
            P("seg", "seq", None),
            P(("seq", "seg")),
            P(("seq", "seg"), None),
            P(("seq", "seg"), None),
            P(("seq", "seg"), None),
            P(("seq", "seg"), None),
            P(("seq", "seg")),
            P("seq", "seg"),
            P("seq", "seg"),
            P(("seq", "seg")),
            P("seq", "seg"),
            P(("seq", "seg")),
            P("seq", "seg"),
            P("seq", "seg"),
        ),
        check_vma=False,
    )
```

profile of v0, /device:TPU:0, one launch (start us, length us, event | category | flops | bytes accessed | tf_op | source)
XLA Modules:
  0.0 3235.0 jit_solution(5679768690738794639)
XLA Ops:
  9.5 10.3 all_gather.94
  19.8 9.4 all-gather.32.cloned.1.call-done
  37.4 10.2 all-gather.40.cloned.1.call-done
  56.4 20.5 all-gather.18
  108.2 21.0 all-gather.21
  129.1 26.3 all-gather.1
  155.4 26.3 all-gather.9
  181.7 27.8 all-gather.3
  209.5 34.4 %all-gather.7 = bf16[1024,16]{0,1:T(8,128)(2,1)S(1)} all-gather(bf16[128,16]{0,1:T(8,128)(2,1)S(1)} %reshape.1259), channel_id=9, replica_groups=mesh['seq'=8,'seg'=4] {'seq'}, dimensions={0}, use_global_device_ids=true | all-gather | bytes 36864 | tf_op jit(solution)/shard_map/all_gather | solution.py:142
  248.0 9.1 fusion.29
  262.9 400.2 %while.60 = (s32[]{:T(128)}, f32[1,128,16]{2,1,0:T(8,128)S(1)}, f32[16,1,128,128]{3,2,1,0:T(8,128)S(1)}, f32[16,1,128,128]{3,2,1,0:T(8,128)}, f32[16,1,128,128,1...) while((s32[]{:T(128)}, f32[1,128,16]{2,1,0:T(8,128)S(1)}, ...), condition=%wide.region_4.5_spmd.clone.clone.clone.clone, body=%wide.region_3.4_spmd.clone.clone.clone.clone.sunk | while | flops 10693764 | bytes 26499972 | solution.py:56
  404.7 8.2 bitcast_dynamic-update-slice_fusion.8
  530.0 8.2 bitcast_dynamic-update-slice_fusion.8
  663.4 8.9 copy.566
  672.3 12.6 reduce.30
  689.7 20.9 all-gather.22
  712.1 18.4 all-reduce.3
  731.1 10.3 reshape.1387
  815.5 8.7 all-to-all-done.2
  836.8 632.4 %while.59 = (s32[]{:T(128)}, f32[128,128,128]{2,1,0:T(8,128)}, f32[128,128,16]{2,1,0:T(8,128)}, f32[128,128,16]{2,1,0:T(8,128)}, f32[128,16]{1,0:T(8,128)S(1)}, ...) while((s32[]{:T(128)}, f32[128,128,128]{2,1,0:T(8,128)}, ...), condition=%wide.region_12.13_spmd.clone.clone.clone, body=%wide.region_11.12_spmd.clone.clone.clone.sunk | while | flops 16283652 | bytes 31193056 | solution.py:56
  844.8 8.9 bitcast_add_fusion.12
  875.0 15.5 bitcast_add_fusion.12
  915.1 15.5 bitcast_add_fusion.12
  955.3 15.5 bitcast_add_fusion.12
  995.4 15.5 bitcast_add_fusion.12
  1035.6 15.5 bitcast_add_fusion.12
  1075.7 15.5 bitcast_add_fusion.12
  1115.9 15.5 bitcast_add_fusion.12
  1156.0 15.5 bitcast_add_fusion.12
  1196.1 15.5 bitcast_add_fusion.12
  1236.3 15.5 bitcast_add_fusion.12
  1276.4 15.5 bitcast_add_fusion.12
  1316.6 15.5 bitcast_add_fusion.12
  1356.7 15.5 bitcast_add_fusion.12
  1396.8 15.5 bitcast_add_fusion.12
  1437.0 15.5 bitcast_add_fusion.12
  1477.3 12.5 multiply_reduce_fusion.5
  1516.1 10.0 fusion.112
  1526.2 10.6 fusion.78
  1536.8 10.2 fusion.77
  1550.6 8.3 copy.565
  1558.9 12.3 reduce.32
  1581.2 37.3 %reduce-scatter.45.cloned.1.call-done = f32[1,128,16]{1,2,0:T(8,128)} async-done(((f32[8,128,16]{1,2,0:T(8,128)}), f32[1,128,16]{1,2,0:T(8,128)}) %reduce-scatter.45.cloned.1.call-update) | async-done | bytes 8208 | tf_op jit(solution)/shard_map/reduce_scatter | solution.py:362
  1620.0 62.8 %reduce-scatter.43.cloned.1.call-done = f32[1,128,16]{1,2,0:T(8,128)} async-done(((f32[8,128,16]{1,2,0:T(8,128)}), f32[1,128,16]{1,2,0:T(8,128)}) %reduce-scatter.43.cloned.1.call-update) | async-done | bytes 8208 | tf_op jit(solution)/shard_map/reduce_scatter | solution.py:361
  1684.2 62.5 %reduce-scatter.41.cloned.1.call-done = f32[1,128,16]{1,2,0:T(8,128)} async-done(((f32[8,128,16]{1,2,0:T(8,128)}), f32[1,128,16]{1,2,0:T(8,128)}) %reduce-scatter.41.cloned.1.call-update) | async-done | bytes 8208 | tf_op jit(solution)/shard_map/reduce_scatter | solution.py:360
  1755.9 37.3 %all-reduce.9 = (bf16[8,128]{1,0:T(8,128)(2,1)S(1)}, bf16[8,128]{1,0:T(8,128)(2,1)S(1)}, bf16[8,64]{1,0:T(8,128)(2,1)S(1)}, bf16[8,128]{1,0:T(8,128)(2,1)S(1)}) all-reduce(f32[8,128]{1,0:T(8,128)S(1)} %bitcast.639, f32[8,128]{1,0:T(8,128)S(1)} %bitcast.625, ...), channel_id=18, replica_groups=mesh['seq'=8,'seg'=4] {'seq'}, use_global_device_ids=true, to_apply=%region_15.16.clone | all-reduce | flops 3584 | bytes 21504
  1799.0 100.0 %reduce-scatter.55.cloned.1.call-done = f32[256,1024]{1,0:T(8,128)} async-done(((f32[2048,1024]{1,0:T(8,128)}), f32[256,1024]{1,0:T(8,128)}) %reduce-scatter.55.cloned.1.call-update) | async-done | bytes 1048592 | tf_op jit(solution)/shard_map/reduce_scatter | solution.py:368
  1901.2 149.8 %reduce-scatter.51.cloned.1.call-done = f32[128,2048]{1,0:T(8,128)} async-done(((f32[1024,2048]{1,0:T(8,128)}), f32[128,2048]{1,0:T(8,128)}) %reduce-scatter.51.cloned.1.call-update) | async-done | bytes 1048592 | tf_op jit(solution)/shard_map/reduce_scatter | solution.py:366
  2053.1 283.2 %reduce-scatter.59.cloned.1.call-done = f32[128,4096]{1,0:T(8,128)} async-done(((f32[1024,4096]{1,0:T(8,128)}), f32[128,4096]{1,0:T(8,128)}) %reduce-scatter.59.cloned.1.call-update) | async-done | bytes 2097168 | tf_op jit(solution)/shard_map/reduce_scatter | solution.py:370
  2339.1 283.2 %reduce-scatter.63.cloned.1.call-done = f32[512,1024]{1,0:T(8,128)} async-done(((f32[4096,1024]{1,0:T(8,128)}), f32[512,1024]{1,0:T(8,128)}) %reduce-scatter.63.cloned.1.call-update) | async-done | bytes 2097168 | tf_op jit(solution)/shard_map/reduce_scatter | solution.py:371
  2625.1 292.6 %reduce-scatter.49.cloned.1.call-done = f32[128,4224]{1,0:T(8,128)} async-done(((f32[1024,4224]{1,0:T(8,128)}), f32[128,4224]{1,0:T(8,128)}) %reduce-scatter.49.cloned.1.call-update) | async-done | bytes 2162704 | tf_op jit(solution)/shard_map/reduce_scatter | solution.py:365
  2928.9 9.7 reduce-scatter.75.cloned.1.call-done
  2940.2 20.7 reduce-scatter.73.cloned.1.call-done
  2962.5 20.7 reduce-scatter.71.cloned.1.call-done
  2984.9 20.8 reduce-scatter.69.cloned.1.call-done
  3010.4 17.1 reduce-scatter.81.cloned.1.call-done
  3028.8 20.5 reduce-scatter.83.cloned.1.call-done
  3050.1 21.0 reduce-scatter.77.cloned.1.call-done
  3071.8 21.6 reduce-scatter.67.cloned.1.call-done
  3095.7 22.4 reduce-scatter.57.cloned.1.call-done
  3119.8 23.0 reduce-scatter.53.cloned.1.call-done
  3144.4 26.0 reduce-scatter.61.cloned.1.call-done
  3172.2 25.6 reduce-scatter.65.cloned.1.call-done
  3199.6 26.0 reduce-scatter.79.cloned.1.call-done
  (1221 shorter events, 1023.4 us)
Async XLA Ops:
  7.2 40.5 %copy-start.84 = (u32[32]{0:T(128)S(1)}, u32[32]{0:T(128)}, u32[]{:S(2)}) copy-start(u32[32]{0:T(128)} %constant.153) | copy-start | bytes 388
  7.2 42.4 %copy-start.80 = (bf16[32]{0:T(256)(128)(2,1)S(1)}, bf16[32]{0:T(256)(128)(2,1)}, u32[]{:S(2)}) copy-start(bf16[32]{0:T(256)(128)(2,1)} %param.22) | copy-start | bytes 196
  7.2 42.6 %copy-start.81 = (bf16[32]{0:T(256)(128)(2,1)S(1)}, bf16[32]{0:T(256)(128)(2,1)}, u32[]{:S(2)}) copy-start(bf16[32]{0:T(256)(128)(2,1)} %param.27) | copy-start | bytes 196
  7.2 42.8 %copy-start.82 = (bf16[32]{0:T(256)(128)(2,1)S(1)}, bf16[32]{0:T(256)(128)(2,1)}, u32[]{:S(2)}) copy-start(bf16[32]{0:T(256)(128)(2,1)} %param.32) | copy-start | bytes 196
  7.2 43.1 %copy-start.83 = (bf16[16]{0:T(256)(128)(2,1)S(1)}, bf16[16]{0:T(256)(128)(2,1)}, u32[]{:S(2)}) copy-start(bf16[16]{0:T(256)(128)(2,1)} %param.30) | copy-start | bytes 100
  7.2 69.7 %copy-start.5 = (bf16[1,256,1024]{2,1,0:T(8,128)(2,1)S(1)}, bf16[1,256,1024]{2,1,0:T(8,128)(2,1)}, u32[]{:S(2)}) copy-start(bf16[1,256,1024]{2,1,0:T(8,128)(2,1)} %param.20) | copy-start | bytes 1572868
  7.2 22.0 all-gather.32.cloned.1.call-start
  8.0 39.6 %all-gather.40.cloned.1.call-start = ((), (), s32[]{:S(2)}) async-start(), calls=%async_computation.30 | async-start | bytes 1310720 | tf_op jit(solution)/shard_map/all_gather | solution.py:135
  8.7 251.8 %all-gather.44.cloned.1.call-start = ((), (), s32[]{:S(2)}) async-start(), calls=%async_computation.32 | async-start | bytes 1310720 | tf_op jit(solution)/shard_map/all_gather | solution.py:136
  9.5 735.3 %all-gather.36.cloned.1.call-start = ((), (), s32[]{:S(2)}) async-start(), calls=%async_computation.28 | async-start | bytes 4718592 | tf_op jit(solution)/shard_map/all_gather | solution.py:146
  19.8 730.4 %all-gather.34.cloned.1.call-start = ((), (), s32[]{:S(2)}) async-start(), calls=%async_computation.27 | async-start | bytes 9732096 | tf_op jit(solution)/shard_map/all_gather | solution.py:145
  29.3 732.1 %all-gather.38.cloned.1.call-start = ((), (), s32[]{:S(2)}) async-start(), calls=%async_computation.29 | async-start | bytes 4718592 | tf_op jit(solution)/shard_map/all_gather | solution.py:148
  37.3 49.7 %copy-start.65 = (bf16[32,16]{0,1:T(8,128)(2,1)S(1)}, bf16[32,16]{0,1:T(8,128)(2,1)}, u32[]{:S(2)}) copy-start(bf16[32,16]{0,1:T(8,128)(2,1)} %param.23) | copy-start | bytes 3076
  37.3 55.0 %copy-start.66 = (bf16[32,16]{0,1:T(8,128)(2,1)S(1)}, bf16[32,16]{0,1:T(8,128)(2,1)}, u32[]{:S(2)}) copy-start(bf16[32,16]{0,1:T(8,128)(2,1)} %param.26) | copy-start | bytes 3076
  37.3 60.3 %copy-start.67 = (bf16[32,16]{0,1:T(8,128)(2,1)S(1)}, bf16[32,16]{0,1:T(8,128)(2,1)}, u32[]{:S(2)}) copy-start(bf16[32,16]{0,1:T(8,128)(2,1)} %param.24) | copy-start | bytes 3076
  37.3 65.5 %copy-start.68 = (bf16[32,16]{0,1:T(8,128)(2,1)S(1)}, bf16[32,16]{0,1:T(8,128)(2,1)}, u32[]{:S(2)}) copy-start(bf16[32,16]{0,1:T(8,128)(2,1)} %param.25) | copy-start | bytes 3076
  37.4 207.2 %copy-start.72 = (s32[1,4]{1,0:T(1,128)S(1)}, s32[1,4]{1,0:T(1,128)}, u32[]{:S(2)}) copy-start(s32[1,4]{1,0:T(1,128)} %param.21) | copy-start | bytes 52
  37.4 730.0 %all-gather.42.cloned.1.call-start = ((), (), s32[]{:S(2)}) async-start(), calls=%async_computation.31 | async-start | bytes 9437184 | tf_op jit(solution)/shard_map/all_gather | solution.py:150
  76.9 667.9 %copy-start.40 = (f32[8,1,128]{2,1,0:T(1,128)}, f32[8,1,128]{2,1,0:T(1,128)S(1)}, u32[]{:S(2)}) copy-start(f32[8,1,128]{2,1,0:T(1,128)S(1)} %convert_element_type.489) | copy-start | bytes 12292
  77.1 667.7 %copy-start.54 = (f32[256]{0:T(256)}, f32[256]{0:T(256)S(1)}, u32[]{:S(2)}) copy-start(f32[256]{0:T(256)S(1)} %add_rsqrt_fusion.1) | copy-start | bytes 3076
  83.5 173.6 %all-to-all-start = ((bf16[8,2,16384]{2,1,0:T(2,128)(2,1)}), bf16[8,2,16384]{2,1,0:T(2,128)(2,1)S(1)}, u32[]{:S(2)}, u32[]{:S(2)}) async-start(bf16[8,2,16384]{2,1,0:T(2,128)(2,1)} %reshape.1384), calls=%async_computation | async-start | bytes 1048576 | tf_op jit(solution)/shard_map/all_to_all | solution.py:173
  87.0 688.2 %all-gather.46.cloned.1.call-start = ((), (), s32[]{:S(2)}) async-start(), calls=%async_computation.33 | async-start | bytes 9437184 | tf_op jit(solution)/shard_map/all_gather | solution.py:151
  155.4 90.0 %copy-start.42 = (bf16[1024,16]{0,1:T(8,128)(2,1)}, bf16[1024,16]{0,1:T(8,128)(2,1)S(1)}, u32[]{:S(2)}) copy-start(bf16[1024,16]{0,1:T(8,128)(2,1)S(1)} %all-gather.1) | copy-start | bytes 98308
  181.7 63.7 %copy-start.43 = (bf16[1024,16]{0,1:T(8,128)(2,1)}, bf16[1024,16]{0,1:T(8,128)(2,1)S(1)}, u32[]{:S(2)}) copy-start(bf16[1024,16]{0,1:T(8,128)(2,1)S(1)} %all-gather.9) | copy-start | bytes 98308
  209.5 35.9 %copy-start.44 = (bf16[1024,16]{0,1:T(8,128)(2,1)}, bf16[1024,16]{0,1:T(8,128)(2,1)S(1)}, u32[]{:S(2)}) copy-start(bf16[1024,16]{0,1:T(8,128)(2,1)S(1)} %all-gather.3) | copy-start | bytes 98308
  244.0 419.1 %copy-start.60 = (f32[128]{0:T(128)}, f32[128]{0:T(128)S(1)}, u32[]{:S(2)}) copy-start(f32[128]{0:T(128)S(1)} %dynamic-slice_convert_fusion.1) | copy-start | bytes 1540
  663.1 47.5 %copy-start.73 = (u32[32]{0:T(128)S(1)}, u32[32]{0:T(128)}, u32[]{:S(2)}) copy-start(u32[32]{0:T(128)} %constant.168) | copy-start | bytes 388
  685.8 45.3 %all-to-all-start.1 = ((bf16[8,2,16384]{2,1,0:T(2,128)(2,1)}), bf16[8,2,16384]{2,1,0:T(2,128)(2,1)S(1)}, u32[]{:S(2)}, u32[]{:S(2)}) async-start(bf16[8,2,16384]{2,1,0:T(2,128)(2,1)} %reshape.1386), calls=%async_computation.1 | async-start | bytes 1048576 | tf_op jit(solution)/shard_map/all_to_all | solution.py:213
  731.1 25.6 copy-start.63
  767.4 23.9 copy-start.56
  798.7 16.1 copy-start.52
  807.8 25.3 copy-start.61
  809.8 14.4 all-to-all-start.2
  813.9 765.7 %reduce-scatter.47.cloned.1.call-start = ((), (), s32[]{:S(2)}) async-start(), calls=%async_computation.37 | async-start | bytes 73728 | tf_op jit(solution)/shard_map/reduce_scatter | solution.py:363
  915.1 15.6 copy-start.50
  955.3 15.6 copy-start.50
  995.4 15.6 copy-start.50
  1493.0 125.5 %reduce-scatter.45.cloned.1.call-start = ((), (), s32[]{:S(2)}) async-start(), calls=%async_computation.36 | async-start | bytes 73728 | tf_op jit(solution)/shard_map/reduce_scatter | solution.py:362
  1499.5 183.3 %reduce-scatter.43.cloned.1.call-start = ((), (), s32[]{:S(2)}) async-start(), calls=%async_computation.35 | async-start | bytes 73728 | tf_op jit(solution)/shard_map/reduce_scatter | solution.py:361
  1500.3 246.5 %reduce-scatter.41.cloned.1.call-start = ((), (), s32[]{:S(2)}) async-start(), calls=%async_computation.34 | async-start | bytes 73728 | tf_op jit(solution)/shard_map/reduce_scatter | solution.py:360
  1501.0 398.1 %reduce-scatter.55.cloned.1.call-start = ((), (), s32[]{:S(2)}) async-start(), calls=%async_computation.41 | async-start | bytes 9437184 | tf_op jit(solution)/shard_map/reduce_scatter | solution.py:368
  1507.1 543.9 %reduce-scatter.51.cloned.1.call-start = ((), (), s32[]{:S(2)}) async-start(), calls=%async_computation.39 | async-start | bytes 9437184 | tf_op jit(solution)/shard_map/reduce_scatter | solution.py:366
  1516.1 820.3 %reduce-scatter.59.cloned.1.call-start = ((), (), s32[]{:S(2)}) async-start(), calls=%async_computation.43 | async-start | bytes 18874368 | tf_op jit(solution)/shard_map/reduce_scatter | solution.py:370
  1526.1 1096.2 %reduce-scatter.63.cloned.1.call-start = ((), (), s32[]{:S(2)}) async-start(), calls=%async_computation.45 | async-start | bytes 18874368 | tf_op jit(solution)/shard_map/reduce_scatter | solution.py:371
  1536.8 1381.0 %reduce-scatter.49.cloned.1.call-start = ((), (), s32[]{:S(2)}) async-start(), calls=%async_computation.38 | async-start | bytes 19464192 | tf_op jit(solution)/shard_map/reduce_scatter | solution.py:365
  1550.6 26.9 copy-start.17
  1573.2 175.1 %all-to-all-start.3 = ((bf16[8,2,16384]{2,1,0:T(2,128)(2,1)}), bf16[8,2,16384]{2,1,0:T(2,128)(2,1)}, u32[]{:S(2)}, u32[]{:S(2)}) async-start(bf16[8,2,16384]{2,1,0:T(2,128)(2,1)} %reshape.1390), calls=%async_computation.3 | async-start | bytes 1048576 | tf_op jit(solution)/shard_map/all_to_all | solution.py:324
  1577.4 1361.2 %reduce-scatter.75.cloned.1.call-start = ((), (), s32[]{:S(2)}) async-start(), calls=%async_computation.51 | async-start | bytes 40960
  1577.4 174.1 %copy-start.8 = (bf16[1,256,1024]{2,1,0:T(8,128)(2,1)S(1)}, bf16[1,256,1024]{2,1,0:T(8,128)(2,1)}, u32[]{:S(2)}) copy-start(bf16[1,256,1024]{2,1,0:T(8,128)(2,1)} %param.20) | copy-start | bytes 1572868
  1581.1 1379.8 %reduce-scatter.73.cloned.1.call-start = ((), (), s32[]{:S(2)}) async-start(), calls=%async_computation.50 | async-start | bytes 40960
  1619.9 1363.3 %reduce-scatter.71.cloned.1.call-start = ((), (), s32[]{:S(2)}) async-start(), calls=%async_computation.49 | async-start | bytes 40960
  1684.2 1321.5 %reduce-scatter.69.cloned.1.call-start = ((), (), s32[]{:S(2)}) async-start(), calls=%async_computation.48 | async-start | bytes 40960
  1748.2 1279.3 %reduce-scatter.81.cloned.1.call-start = ((), (), s32[]{:S(2)}) async-start(), calls=%async_computation.54 | async-start | bytes 20480
  1794.6 1254.7 %reduce-scatter.83.cloned.1.call-start = ((), (), s32[]{:S(2)}) async-start(), calls=%async_computation.55 | async-start | bytes 40960
  1796.0 1275.0 %reduce-scatter.77.cloned.1.call-start = ((), (), s32[]{:S(2)}) async-start(), calls=%async_computation.52 | async-start | bytes 40960
  1797.5 1295.9 %reduce-scatter.67.cloned.1.call-start = ((), (), s32[]{:S(2)}) async-start(), calls=%async_computation.47 | async-start | bytes 40960
  1799.0 1319.2 %reduce-scatter.57.cloned.1.call-start = ((), (), s32[]{:S(2)}) async-start(), calls=%async_computation.42 | async-start | bytes 655360 | tf_op jit(solution)/shard_map/reduce_scatter | solution.py:401
  1901.2 1241.6 %reduce-scatter.53.cloned.1.call-start = ((), (), s32[]{:S(2)}) async-start(), calls=%async_computation.40 | async-start | bytes 655360 | tf_op jit(solution)/shard_map/reduce_scatter | solution.py:395
  2053.1 1117.3 %reduce-scatter.61.cloned.1.call-start = ((), (), s32[]{:S(2)}) async-start(), calls=%async_computation.44 | async-start | bytes 1310720 | tf_op jit(solution)/shard_map/reduce_scatter | solution.py:407
  2339.1 858.8 %reduce-scatter.65.cloned.1.call-start = ((), (), s32[]{:S(2)}) async-start(), calls=%async_computation.46 | async-start | bytes 1310720 | tf_op jit(solution)/shard_map/reduce_scatter | solution.py:410
  2625.1 600.5 %reduce-scatter.79.cloned.1.call-start = ((), (), s32[]{:S(2)}) async-start(), calls=%async_computation.53 | async-start | bytes 1351680
  2920.9 86.3 %copy-start.16 = (f32[256,1024]{1,0:T(8,128)S(1)}, f32[256,1024]{1,0:T(8,128)}, u32[]{:S(2)}) copy-start(f32[256,1024]{1,0:T(8,128)} %copy-done.15) | copy-start | bytes 3145732
  2921.0 86.3 %copy-start.26 = (bf16[1,256,1024]{2,1,0:T(8,128)(2,1)S(1)}, bf16[1,256,1024]{2,1,0:T(8,128)(2,1)}, u32[]{:S(2)}) copy-start(bf16[1,256,1024]{2,1,0:T(8,128)(2,1)} %param.35) | copy-start | bytes 1572868
  2921.0 86.3 %copy-start.59 = (f32[256]{0:T(256)S(1)}, f32[256]{0:T(256)}, u32[]{:S(2)}) copy-start(f32[256]{0:T(256)} %copy-done.58) | copy-start | bytes 3076
  (150 other events, 1055.0 us)
Sparse Core Ops, SparseCore 0:
  9.6 19.5 all-gather.31
  30.8 16.7 all-gather.39
  49.2 16.8 all-gather.43
  68.1 84.1 all-gather.35
  154.1 128.4 all-gather.33
  284.6 71.5 all-gather.37
  358.4 123.6 all-gather.41
  484.2 123.1 all-gather.45
  1493.1 62.5 reduce-scatter.46
  1558.9 59.5 reduce-scatter.44
  1622.4 60.2 reduce-scatter.42
  1686.5 60.1 reduce-scatter.40
  1750.4 148.6 reduce-scatter.54
  1903.0 147.9 reduce-scatter.50
  2054.6 281.6 reduce-scatter.58
  2340.4 281.7 reduce-scatter.62
  2626.0 291.6 reduce-scatter.48
  2920.1 18.3 reduce-scatter.74
  2941.6 19.3 reduce-scatter.72
  2963.9 19.3 reduce-scatter.70
  2986.3 19.3 reduce-scatter.68
  3008.2 19.2 reduce-scatter.80
  3029.9 19.3 reduce-scatter.82
  3051.7 19.3 reduce-scatter.76
  3074.0 19.3 reduce-scatter.66
  3096.5 21.6 reduce-scatter.56
  3121.1 21.6 reduce-scatter.52
  3145.5 24.8 reduce-scatter.60
  3173.0 24.8 reduce-scatter.64
  3200.4 25.1 reduce-scatter.78
where the time goes:
time: 3260 us; the launch traced here: 3230 us
  waiting for transfers between devices  1580 us (48%)
  other arithmetic  985 us (30%)
  blocking collectives  278 us (9%)
  local copies, waits for them, and re-layouts  233 us (7%)
  matrix products  114 us (3%)
    reduce_scatter x1, waiting for transfers between devices, body(): lax.psum_scatter(terms[6], 'seq', scatter_dimension=0, tiled=True)  293 us
    reduce_scatter x1, waiting for transfers between devices, body(): lax.psum_scatter(terms[11], 'seq', scatter_dimension=0, tiled=True)  283 us
    reduce_scatter x1, waiting for transfers between devices, body(): lax.psum_scatter(terms[12], 'seq', scatter_dimension=0, tiled=True)  283 us
    add_any x16, other arithmetic, advance(): jnp.einsum('ns,nsc,sch->nch', tail_mask, values, feed_pow, precision=high...  242 us
    dynamic_update_slice x112, other arithmetic, ema_apply(): _, outputs = lax.scan(advance, start_state, (pieces, labels, before))  209 us
    unnamed x39, waiting for transfers between devices  181 us
    dot_general x32, other arithmetic, advance(): jnp.einsum('isc,nis,nsc->nic', toeplitz, same_doc, values, precision=high...  156 us
    reduce_scatter x1, waiting for transfers between devices, body(): lax.psum_scatter(terms[7], 'seq', scatter_dimension=0, tiled=True)  150 us
  transfers between devices with their start and end apart: 34, of which 24 were waited for; matrix products, arithmetic and copies ran while one was open for 19% of the time, Pallas kernels for 0%

commit v1 on v0

v1 whole, which is shorter than its diff:
```python
import functools
import math

import jax
import jax.numpy as jnp
import numpy as np
from jax import lax
from jax.experimental import pallas as pl
from jax.experimental.pallas import tpu as pltpu
from jax.sharding import PartitionSpec as P

STRETCH = 128
epsilon = 1e-05

MESH = pl.DeviceIdType.MESH
ANY = pl.BlockSpec(memory_space=pl.ANY)


class Grid:
    def __init__(self, nq, ng):
        self.nq, self.ng = nq, ng
        self.nz = math.gcd(nq, 4)
        self.nx = nq // self.nz
        self.nc = math.gcd(ng, 2)
        self.ny = ng // self.nc

    def here(self):
        s, g = lax.axis_index("seq"), lax.axis_index("seg")
        return s // self.nx, lax.rem(s, self.nx), g // self.nc, lax.rem(g, self.nc)

    def peer(self, axis, d):
        z, x, y, c = self.here()
        if axis == "z":
            z = lax.rem(z + d, self.nz)
        if axis == "x":
            x = lax.rem(x + d, self.nx)
        if axis == "y":
            y = lax.rem(y + d, self.ny)
        if axis == "c":
            c = lax.rem(c + d, self.nc)
        return z, x, y, c

    def size(self, axis):
        return {"z": self.nz, "x": self.nx, "y": self.ny, "c": self.nc}[axis]

    def device(self, place):
        z, x, y, c = place
        return {"seq": z * self.nx + x, "seg": y * self.nc + c}

    def peers(self, axes):
        return [self.peer(a, d) for a in axes for d in range(1, self.size(a))]


def enter(grid, peers):
    barrier = pltpu.get_barrier_semaphore()
    for place in peers:
        pl.semaphore_signal(barrier, inc=1, device_id=grid.device(place), device_id_type=MESH)
    pl.semaphore_wait(barrier, len(peers))


class Sems:
    def __init__(self, send, recv):
        self.send, self.recv, self.used = send, recv, 0

    def take(self):
        i = self.used
        self.used += 1
        return self.send.at[i], self.recv.at[i]


def gather_kernel(grid, shapes, count, *refs):
    n = len(shapes)
    shards, wholes = refs[:n], refs[n : 2 * n]
    own_sem, send, recv = refs[2 * n :]
    sems = Sems(send, recv)
    z, x, y, c = grid.here()
    enter(grid, grid.peers("zxyc"))
    pending = []

    def push(src, dst, axis, d, arrives):
        s, r = sems.take()
        copy = pltpu.make_async_remote_copy(
            src, dst, s, r, device_id=grid.device(grid.peer(axis, d)), device_id_type=MESH
        )
        copy.start()
        pending.append(copy)
        there = pltpu.make_async_remote_copy(
            arrives, arrives, s, r, device_id=grid.device(grid.peer(axis, d)), device_id_type=MESH
        )
        return there.wait_recv

    def back(axis, d):
        place = grid.peer(axis, grid.size(axis) - d)
        return dict(zip("zxyc", place))

    owns = []
    for i in range(n):
        copy = pltpu.make_async_copy(shards[i], wholes[i].at[y, c, z, x], own_sem.at[i])
        copy.start()
        owns.append(copy)

    chunks = [(i, q) for i in range(n) for q in range(shapes[i][0] // 2)]
    halves = (0, 1)
    core_waits = []

    def core(view):
        core_waits.extend(
            push(view(c), view(c), "c", d, view(back("c", d)["c"])) for d in range(1, grid.nc)
        )

    def stage_z(i, h):
        w = wholes[i]
        return [
            push(shards[i].at[h], w.at[y, c, z, x, h], "z", d, w.at[y, c, back("z", d)["z"], x, h])
            for d in range(1, grid.nz)
        ]

    def stage_two(i, h):
        w = wholes[i]
        core(lambda cc: w.at[y, cc, :, x, h])
        src = w.at[y, c, :, x, h]
        if h % 2 == 0:
            return [push(src, src, "x", d, w.at[y, c, :, back("x", d)["x"], h]) for d in range(1, grid.nx)]
        return [push(src, src, "y", d, w.at[back("y", d)["y"], c, :, x, h]) for d in range(1, grid.ny)]

    def stage_three(i, h):
        w = wholes[i]
        if h % 2 == 0:
            for d in range(1, grid.nx):
                core(lambda cc: w.at[y, cc, :, back("x", d)["x"], h])
            src = w.at[y, c, :, :, h]
            return [push(src, src, "y", d, w.at[back("y", d)["y"], c, :, :, h]) for d in range(1, grid.ny)]
        for d in range(1, grid.ny):
            core(lambda cc: w.at[back("y", d)["y"], cc, :, x, h])
        src = w.at[:, c, :, x, h]
        return [push(src, src, "x", d, w.at[:, c, :, back("x", d)["x"], h]) for d in range(1, grid.nx)]

    def stage_last(i, h):
        w = wholes[i]
        if h % 2 == 0:
            for d in range(1, grid.ny):
                core(lambda cc: w.at[back("y", d)["y"], cc, :, :, h])
        else:
            for d in range(1, grid.nx):
                core(lambda cc: w.at[:, cc, :, back("x", d)["x"], h])

    def finish(waits):
        for wait in waits:
            wait()

    got_z, got_two, got_three = {}, {}, {}
    ahead = 2
    total = len(chunks)
    for t in range(total + 3 + ahead):
        k = t
        if k < total:
            i, q = chunks[k]
            for h in halves:
                got_z[k, h] = stage_z(i, 2 * q + h)
        k = t - ahead
        if 0 <= k < total:
            i, q = chunks[k]
            if q == 0:
                owns[i].wait()
            for h in halves:
                finish(got_z[k, h])
                got_two[k, h] = stage_two(i, 2 * q + h)
        k = t - ahead - 1
        if 0 <= k < total:
            i, q = chunks[k]
            for h in halves:
                finish(got_two[k, h])
                got_three[k, h] = stage_three(i, 2 * q + h)
        k = t - ahead - 2
        if 0 <= k < total:
            i, q = chunks[k]
            for h in halves:
                finish(got_three[k, h])
                stage_last(i, 2 * q + h)
    finish(core_waits)
    for copy in pending:
        copy.wait_send()
    assert sems.used <= count, sems.used


def gather_all(grid, shards, cuts, collective_id):
    shapes, args, outs = [], [], []
    for w, q in zip(shards, cuts):
        k, n = w.shape
        shapes.append((2 * q, k // (2 * q), n))
        args.append(w.reshape(shapes[-1]))
        outs.append(jax.ShapeDtypeStruct((grid.ny, grid.nc, grid.nz, grid.nx) + shapes[-1], w.dtype))
    per = (grid.nz - 1) + (grid.nx - 1) + (grid.ny - 1) + (grid.nc - 1) * (grid.nx + grid.ny)
    count = sum(s[0] for s in shapes) * per
    wholes = pl.pallas_call(
        functools.partial(gather_kernel, grid, shapes, count),
        out_shape=outs,
        in_specs=[ANY] * len(args),
        out_specs=[ANY] * len(args),
        scratch_shapes=[
            pltpu.SemaphoreType.DMA((len(args),)),
            pltpu.SemaphoreType.DMA((count,)),
            pltpu.SemaphoreType.DMA((count,)),
        ],
        compiler_params=pltpu.CompilerParams(collective_id=collective_id, has_side_effects=True),
    )(*args)
    return [w.reshape(grid.ng, -1, w.shape[-1]) for w in wholes]


def scatter_kernel(grid, shapes, count, *refs):
    n = len(shapes)
    nz, nx, ny, nc = grid.nz, grid.nx, grid.ny, grid.nc
    nq, ng = grid.nq, grid.ng
    small, refs = refs[0], refs[1:]
    terms, sums = refs[:n], refs[n : 2 * n]
    small_sum, small_seq, small_seg, s_send, s_recv = refs[2 * n : 2 * n + 5]
    scratch = refs[2 * n + 5 :]
    own = [scratch[7 * i] for i in range(n)]
    one = [scratch[7 * i + 1] for i in range(n)]
    two_a = [scratch[7 * i + 2] for i in range(n)]
    two_b = [scratch[7 * i + 3] for i in range(n)]
    three_a = [scratch[7 * i + 4] for i in range(n)]
    three_b = [scratch[7 * i + 5] for i in range(n)]
    four = [scratch[7 * i + 6] for i in range(n)]
    own_sem, send, recv = scratch[7 * n :]
    sems = Sems(send, recv)
    z, x, y, c = grid.here()
    sq, sg = lax.axis_index("seq"), lax.axis_index("seg")
    seq_peer = [{"seq": lax.rem(sq + d, nq), "seg": sg} for d in range(1, nq)]
    seg_peer = [{"seq": sq, "seg": lax.rem(sg + d, ng)} for d in range(1, ng)]
    barrier = pltpu.get_barrier_semaphore()
    for place in seq_peer + seg_peer:
        pl.semaphore_signal(barrier, inc=1, device_id=place, device_id_type=MESH)
    pl.semaphore_wait(barrier, nq + ng - 2)
    pending = []

    small_copies = []
    for d in range(1, nq):
        small_copies.append(pltpu.make_async_remote_copy(
            small.at[lax.rem(sq + d, nq)], small_seq.at[d - 1], s_send.at[d - 1], s_recv.at[d - 1],
            device_id=seq_peer[d - 1], device_id_type=MESH))
        small_copies[-1].start()

    def small_middle():
        total = small[sq]
        for d in range(1, nq):
            small_copies[d - 1].wait_recv()
            total += small_seq[d - 1]
        small_sum[...] = total
        for d in range(1, ng):
            small_copies.append(pltpu.make_async_remote_copy(
                small_sum, small_seg.at[d - 1], s_send.at[nq + d - 2], s_recv.at[nq + d - 2],
                device_id=seg_peer[d - 1], device_id_type=MESH))
            small_copies[-1].start()

    def small_end():
        total = small_sum[...]
        for d in range(1, ng):
            small_copies[nq + d - 2].wait_recv()
            total += small_seg[d - 1]
        for copy in small_copies:
            copy.wait_send()
        small_sum[...] = total

    def push(src, dst, axis, d):
        s, r = sems.take()
        copy = pltpu.make_async_remote_copy(
            src, dst, s, r, device_id=grid.device(grid.peer(axis, d)), device_id_type=MESH
        )
        copy.start()
        pending.append(copy)
        return copy.wait_recv

    def to(axis, d):
        return dict(zip("zxyc", grid.peer(axis, d)))[axis]

    def finish(waits):
        for wait in waits:
            wait()

    assert nc == 2

    def stage_one(i, q, h):
        return [push(terms[i].at[:, to("c", 1), :, :, 2 * q + h], one[i].at[q, h], "c", 1)]

    def load_own(i, q, h):
        load = pltpu.make_async_copy(terms[i].at[:, c, :, :, 2 * q + h], own[i].at[h], own_sem.at[i, h])
        load.start()
        return [load.wait]

    def stage_two(i, q, h):
        mine = one[i].at[q, h]

        @pl.loop(0, ny * nz)
        def _(ab):
            a, b = ab // nz, lax.rem(ab, nz)
            for e in range(nx):
                mine[a, b, e] += own[i][h, a, b, e]

        if h == 0:
            return [push(mine.at[to("y", d)], two_a[i].at[q, d - 1], "y", d) for d in range(1, ny)]
        return [push(mine.at[:, :, to("x", d)], two_b[i].at[q, d - 1], "x", d) for d in range(1, nx)]

    def stage_three(i, q, h):
        mine = one[i].at[q, h]
        if h == 0:

            @pl.loop(0, nz)
            def _(b):
                for e in range(nx):
                    total = mine[y, b, e]
                    for d in range(ny - 1):
                        total += two_a[i][q, d, b, e]
                    mine[y, b, e] = total

            return [push(mine.at[y, :, to("x", d)], three_a[i].at[q, d - 1], "x", d) for d in range(1, nx)]

        @pl.loop(0, nz)
        def _(b):
            for a in range(ny):
                total = mine[a, b, x]
                for d in range(nx - 1):
                    total += two_b[i][q, d, a, b]
                mine[a, b, x] = total

        return [push(mine.at[to("y", d), :, x], three_b[i].at[q, d - 1], "y", d) for d in range(1, ny)]

    def stage_four(i, q, h):
        mine = one[i].at[q, h]
        came = three_a[i] if h == 0 else three_b[i]

        @pl.loop(0, nz)
        def _(b):
            total = mine[y, b, x]
            for d in range((nx if h == 0 else ny) - 1):
                total += came[q, d, b]
            mine[y, b, x] = total

        return [push(mine.at[y, to("z", d), x], four[i].at[q, h, d - 1], "z", d) for d in range(1, nz)]

    def stage_last(i, q, h):
        total = one[i][q, h, y, z, x].astype(jnp.float32)
        for d in range(nz - 1):
            total += four[i][q, h, d].astype(jnp.float32)
        sums[i][2 * q + h] = total

    stages = [stage_one, stage_two, stage_three, stage_four, stage_last]
    chunks = [(i, q) for i in range(n) for q in range(shapes[i][0] // 2)]
    waits = {}
    for t in range(len(chunks) + len(stages) - 1):
        if t == 1:
            small_middle()
        for j, stage in enumerate(stages):
            if 0 <= t - j < len(chunks):
                i, q = chunks[t - j]
                for h in (0, 1):
                    if j:
                        finish(waits[i, q, h])
                    waits[i, q, h] = stage(i, q, h)
            if j == 1 and t < len(chunks):
                i, q = chunks[t]
                for h in (0, 1):
                    waits[i, q, h] += load_own(i, q, h)
    small_end()
    for copy in pending:
        copy.wait_send()
    assert sems.used <= count, sems.used


def scatter_all(grid, small, terms, cuts, collective_id, vmem):
    nz, nx, ny, nc = grid.nz, grid.nx, grid.ny, grid.nc
    shapes, args, outs, scratch = [], [], [], []
    for t, q in zip(terms, cuts):
        _, rows, n = t.shape
        kh = rows // grid.nq // (2 * q)
        shapes.append((2 * q, kh, n))
        args.append(t.reshape(ny, nc, nz, nx, 2 * q, kh, n))
        outs.append(jax.ShapeDtypeStruct((2 * q, kh, n), jnp.float32))
        b = t.dtype
        scratch += [
            pltpu.VMEM((2, ny, nz, nx, kh, n), b),
            pltpu.VMEM((q, 2, ny, nz, nx, kh, n), b),
            pltpu.VMEM((q, max(ny - 1, 1), nz, nx, kh, n), b),
            pltpu.VMEM((q, max(nx - 1, 1), ny, nz, kh, n), b),
            pltpu.VMEM((q, max(nx - 1, 1), nz, kh, n), b),
            pltpu.VMEM((q, max(ny - 1, 1), nz, kh, n), b),
            pltpu.VMEM((q, 2, max(nz - 1, 1), kh, n), b),
        ]
    per = (nc - 1) + (nx - 1) + (ny - 1) + (nz - 1)
    count = per * sum(s[0] for s in shapes)
    sums = pl.pallas_call(
        functools.partial(scatter_kernel, grid, shapes, count),
        out_shape=outs + [jax.ShapeDtypeStruct(small.shape[1:], small.dtype)],
        in_specs=[pl.BlockSpec(memory_space=pltpu.VMEM)] + [ANY] * len(args),
        out_specs=[pl.BlockSpec(memory_space=pltpu.VMEM)] * (len(args) + 1),
        scratch_shapes=[
            pltpu.VMEM((grid.nq - 1,) + small.shape[1:], small.dtype),
            pltpu.VMEM((grid.ng - 1,) + small.shape[1:], small.dtype),
            pltpu.SemaphoreType.DMA((grid.nq + grid.ng - 2,)),
            pltpu.SemaphoreType.DMA((grid.nq + grid.ng - 2,)),
        ]
        + scratch
        + [
            pltpu.SemaphoreType.DMA((len(args), 2)),
            pltpu.SemaphoreType.DMA((count,)),
            pltpu.SemaphoreType.DMA((count,)),
        ],
        compiler_params=pltpu.CompilerParams(
            collective_id=collective_id, has_side_effects=True, vmem_limit_bytes=vmem
        ),
    )(small, *args)
    return sums[-1], [s.reshape(-1, s.shape[-1]) for s in sums[:-1]]


def block_of(e, nq, blocks):
    return e * blocks // nq


def mix_kernel(grid, width, dims, *refs):
    (tok, tile, alive, spans, normed_out, active_out, x_out, mixed_out, carry_out, par_out, aff_out,
     tiles, table, bound, sends_t, recv_t, sends_b, recv_b) = refs
    nq, ng = grid.nq, grid.ng
    rows = tok.shape[0]
    blocks = width // 128
    s, g = lax.axis_index("seq"), lax.axis_index("seg")
    seq_peer = [{"seq": lax.rem(s + d, nq), "seg": g} for d in range(1, nq)]
    seg_peer = [{"seq": s, "seg": lax.rem(g + d, ng)} for d in range(1, ng)]
    barrier = pltpu.get_barrier_semaphore()
    for place in seq_peer + seg_peer:
        pl.semaphore_signal(barrier, inc=1, device_id=place, device_id_type=MESH)
    pl.semaphore_wait(barrier, nq + ng - 2)

    copies = []
    for d in range(1, ng):
        copies.append(pltpu.make_async_remote_copy(
            tile, tiles.at[d - 1], sends_t.at[d - 1], recv_t.at[d - 1],
            device_id=seg_peer[d - 1], device_id_type=MESH))
        copies[-1].start()
    for copy in copies:
        copy.wait_recv()
    lanes = tile[...]
    for d in range(1, ng):
        lanes += tiles[d - 1]
    table[s] = lanes
    for d in range(1, nq):
        copies.append(pltpu.make_async_remote_copy(
            table.at[s], table.at[s], sends_t.at[ng + d - 2], recv_t.at[ng + d - 2],
            device_id=seq_peer[d - 1], device_id_type=MESH))
        copies[-1].start()
    for d in range(1, nq):
        came = table.at[lax.rem(s + nq - d, nq)]
        pltpu.make_async_remote_copy(
            came, came, sends_t.at[ng + d - 2], recv_t.at[ng + d - 2],
            device_id=seq_peer[d - 1], device_id_type=MESH).wait_recv()
    count = 4 * dims + 3
    for b in range(blocks):
        mine = [e for e in range(nq) if block_of(e, nq, blocks) == b]
        whole = table[mine[0], 0:count]
        for e in mine[1:]:
            whole += table[e, 0:count]
        par_out[:, b, :] = whole
    aff = table[0, count : count + 4]
    for e in range(1, nq):
        aff += table[e, count : count + 4]
    aff_out[...] = aff

    gain = [par_out[4 * dims, b : b + 1, :] for b in range(blocks)]
    step_rows = 32

    @pl.loop(0, rows // step_rows)
    def _(i):
        at = pl.ds(pl.multiple_of(i * step_rows, step_rows), step_rows)
        v = tok[at, :].astype(jnp.float32)
        r = lax.rsqrt(jnp.mean(v * v, axis=1, keepdims=True) + epsilon)
        for b in range(blocks):
            lane = slice(b * 128, b * 128 + 128)
            n = (v[:, lane] * r * gain[b]).astype(jnp.bfloat16)
            normed_out[at, lane] = n
            x_out[pl.ds(i * step_rows * blocks + b, step_rows, stride=blocks), :] = n.astype(jnp.float32)

    damping = [jax.nn.sigmoid(par_out[j]) for j in range(dims)]
    keep = [1.0 - damping[j] * jax.nn.sigmoid(par_out[dims + j]) for j in range(dims)]
    weight = [damping[j] * par_out[2 * dims + j] * par_out[3 * dims + j] for j in range(dims)]
    omega = par_out[4 * dims + 1]

    def row(ref, p):
        return ref[pl.ds(pl.multiple_of(p * blocks, blocks), blocks), :]

    def first_pass(p, state):
        x, a = row(x_out, p), alive[pl.ds(p, 1), :]
        return tuple(keep[j] * (state[j] * a) + x for j in range(dims))

    zero = tuple(jnp.zeros((blocks, 128), jnp.float32) for _ in range(dims))
    ends = lax.fori_loop(0, rows, first_pass, zero, unroll=4)
    for j in range(dims):
        bound[s, j] = ends[j]
    out = []
    for d in range(1, nq):
        out.append(pltpu.make_async_remote_copy(
            bound.at[s], bound.at[s], sends_b.at[d - 1], recv_b.at[d - 1],
            device_id=seq_peer[d - 1], device_id_type=MESH))
        out[-1].start()
    for d in range(1, nq):
        came = bound.at[lax.rem(s + nq - d, nq)]
        pltpu.make_async_remote_copy(
            came, came, sends_b.at[d - 1], recv_b.at[d - 1],
            device_id=seq_peer[d - 1], device_id_type=MESH).wait_recv()
    for j in range(dims):
        through = power(keep[j], rows)
        state = jnp.zeros((blocks, 128), jnp.float32)
        for e in range(nq - 1):
            later = through * spans[e : e + 1, :] * state + bound[e, j]
            state = jnp.where(e < s, later, state)
        carry_out[j] = state

    def second_pass(p, state):
        x, a = row(x_out, p), alive[pl.ds(p, 1), :]
        state = tuple(keep[j] * (state[j] * a) + x for j in range(dims))
        sums = [omega * x] + [weight[j] * state[j] for j in range(dims)]
        while len(sums) > 1:
            sums = [sum(sums[k : k + 2][1:], sums[k]) for k in range(0, len(sums), 2)]
        mixed_out[pl.ds(pl.multiple_of(p * blocks, blocks), blocks), :] = sums[0]
        return state

    lax.fori_loop(0, rows, second_pass, tuple(carry_out[j] for j in range(dims)), unroll=4)
    for b in range(blocks):
        m = mixed_out[pl.ds(b, rows, stride=blocks), :]
        active_out[:, b * 128 : b * 128 + 128] = (m * jax.nn.sigmoid(m)).astype(jnp.bfloat16)
    for copy in copies + out:
        copy.wait_send()


def power(v, n):
    result = None
    while n:
        if n & 1:
            result = v if result is None else result * v
        n >>= 1
        if n:
            v = v * v
    return result


def mix_forward(grid, tok, tile, alive, spans, dims, collective_id):
    rows, width = tok.shape
    nq, ng = grid.nq, grid.ng
    blocks = width // 128
    f = jnp.float32
    vm = pl.BlockSpec(memory_space=pltpu.VMEM)
    return pl.pallas_call(
        functools.partial(mix_kernel, grid, width, dims),
        out_shape=[
            jax.ShapeDtypeStruct((rows, width), jnp.bfloat16),
            jax.ShapeDtypeStruct((rows, width), jnp.bfloat16),
            jax.ShapeDtypeStruct((rows * blocks, 128), f),
            jax.ShapeDtypeStruct((rows * blocks, 128), f),
            jax.ShapeDtypeStruct((dims, blocks, 128), f),
            jax.ShapeDtypeStruct((4 * dims + 3, blocks, 128), f),
            jax.ShapeDtypeStruct((4, 128), f),
        ],
        in_specs=[vm] * 4,
        out_specs=[vm] * 7,
        scratch_shapes=[
            pltpu.VMEM((ng - 1,) + tile.shape, f),
            pltpu.VMEM((nq,) + tile.shape, f),
            pltpu.VMEM((nq, dims, blocks, 128), f),
            pltpu.SemaphoreType.DMA((nq + ng - 2,)),
            pltpu.SemaphoreType.DMA((nq + ng - 2,)),
            pltpu.SemaphoreType.DMA((nq - 1,)),
            pltpu.SemaphoreType.DMA((nq - 1,)),
        ],
        compiler_params=pltpu.CompilerParams(
            collective_id=collective_id, has_side_effects=True, vmem_limit_bytes=40 << 20
        ),
    )(tok, tile, alive, spans)


def mix_back_kernel(grid, dims, *refs):
    (gact, x_in, mixed, carry, par, alive, spans, gin_out, m_out, k_out, om_out,
     g_rows, gin_rows, before, bound, sends_b, recv_b) = refs
    nq = grid.nq
    rows, width = gact.shape
    blocks = width // 128
    s, g = lax.axis_index("seq"), lax.axis_index("seg")
    seq_peer = [{"seq": lax.rem(s + d, nq), "seg": g} for d in range(1, nq)]
    barrier = pltpu.get_barrier_semaphore()
    for place in seq_peer:
        pl.semaphore_signal(barrier, inc=1, device_id=place, device_id_type=MESH)
    pl.semaphore_wait(barrier, nq - 1)
    for b in range(blocks):
        g_rows[pl.ds(b, rows, stride=blocks), :] = gact[:, b * 128 : b * 128 + 128].astype(jnp.float32)

    @pl.loop(0, rows * blocks // 64)
    def _(i):
        at = pl.ds(pl.multiple_of(i * 64, 64), 64)
        g_rows[at, :] = g_rows[at, :] * silu_slope(mixed[at, :])

    damping = [jax.nn.sigmoid(par[j]) for j in range(dims)]
    keep = [1.0 - damping[j] * jax.nn.sigmoid(par[dims + j]) for j in range(dims)]
    weight = [damping[j] * par[2 * dims + j] * par[3 * dims + j] for j in range(dims)]
    omega = par[4 * dims + 1]

    def row(ref, p):
        return ref[pl.ds(pl.multiple_of(p * blocks, blocks), blocks), :]

    def first_pass(i, flow):
        p = rows - 1 - i
        gp, a = row(g_rows, p), alive[pl.ds(p, 1), :]
        return tuple(keep[j] * (a * (gp + flow[j])) for j in range(dims))

    zero = jnp.zeros((blocks, 128), jnp.float32)
    ends = lax.fori_loop(0, rows, first_pass, (zero,) * dims, unroll=4)
    for j in range(dims):
        bound[s, j] = ends[j]
    out = []
    for d in range(1, nq):
        out.append(pltpu.make_async_remote_copy(
            bound.at[s], bound.at[s], sends_b.at[d - 1], recv_b.at[d - 1],
            device_id=seq_peer[d - 1], device_id_type=MESH))
        out[-1].start()
    for d in range(1, nq):
        came = bound.at[lax.rem(s + nq - d, nq)]
        pltpu.make_async_remote_copy(
            came, came, sends_b.at[d - 1], recv_b.at[d - 1],
            device_id=seq_peer[d - 1], device_id_type=MESH).wait_recv()
    flow_in = []
    for j in range(dims):
        through = power(keep[j], rows)
        flow = zero
        for e in range(nq - 1, 0, -1):
            later = through * spans[e : e + 1, :] * flow + bound[e, j]
            flow = jnp.where(e > s, later, flow)
        flow_in.append(flow)

    few = before.shape[1]
    for j0 in range(0, dims, few):
        js = range(j0, j0 + few)

        def ahead(p, state):
            x, a = row(x_in, p), alive[pl.ds(p, 1), :]
            for t in range(few):
                before[p, t] = state[t]
            return tuple(keep[j] * (state[t] * a) + x for t, j in enumerate(js))

        lax.fori_loop(0, rows, ahead, tuple(carry[j] for j in js), unroll=4)

        def back(i, held):
            flow, m_sum, k_sum, om_sum = held
            p = rows - 1 - i
            at = pl.ds(pl.multiple_of(p * blocks, blocks), blocks)
            gp, x, a = g_rows[at, :], x_in[at, :], alive[pl.ds(p, 1), :]
            total = omega * gp if j0 == 0 else gin_rows[at, :]
            if j0 == 0:
                om_sum = om_sum + gp * x
            new_flow, new_m, new_k = [], [], []
            for t, j in enumerate(js):
                c = gp + flow[t]
                ac = a * c
                total = total + weight[j] * c
                new_flow.append(keep[j] * ac)
                new_m.append(m_sum[t] + c * x)
                new_k.append(k_sum[t] + ac * before[p, t])
            gin_rows[at, :] = total
            return tuple(new_flow), tuple(new_m), tuple(new_k), om_sum

        zeros = (zero,) * few
        _, m_sum, k_sum, om_sum = lax.fori_loop(
            0, rows, back, (tuple(flow_in[j] for j in js), zeros, zeros, zero), unroll=4
        )
        for t, j in enumerate(js):
            m_out[j] = m_sum[t]
            k_out[j] = k_sum[t]
        if j0 == 0:
            om_out[...] = om_sum
    for b in range(blocks):
        gin_out[:, b * 128 : b * 128 + 128] = gin_rows[pl.ds(b, rows, stride=blocks), :].astype(jnp.bfloat16)
    for copy in out:
        copy.wait_send()


def mix_backward(grid, gact, x_in, mixed, carry, par, alive, spans, collective_id):
    rows, width = gact.shape
    nq = grid.nq
    blocks, dims, few = width // 128, carry.shape[0], 4
    f = jnp.float32
    vm = pl.BlockSpec(memory_space=pltpu.VMEM)
    return pl.pallas_call(
        functools.partial(mix_back_kernel, grid, dims),
        out_shape=[
            jax.ShapeDtypeStruct((rows, width), jnp.bfloat16),
            jax.ShapeDtypeStruct((dims, blocks, 128), f),
            jax.ShapeDtypeStruct((dims, blocks, 128), f),
            jax.ShapeDtypeStruct((blocks, 128), f),
        ],
        in_specs=[vm] * 7,
        out_specs=[vm] * 4,
        scratch_shapes=[
            pltpu.VMEM((rows * blocks, 128), f),
            pltpu.VMEM((rows * blocks, 128), f),
            pltpu.VMEM((rows, few, blocks, 128), f),
            pltpu.VMEM((nq, dims, blocks, 128), f),
            pltpu.SemaphoreType.DMA((nq - 1,)),
            pltpu.SemaphoreType.DMA((nq - 1,)),
        ],
        compiler_params=pltpu.CompilerParams(
            collective_id=collective_id, has_side_effects=True, vmem_limit_bytes=40 << 20
        ),
    )(gact, x_in, mixed, carry, par, alive, spans)


def rms_forward(values, gain):
    inverse = lax.rsqrt(jnp.mean(values * values, axis=-1, keepdims=True) + epsilon)
    return (values * inverse * gain, inverse)


def rms_backward(grad_out, values, inverse, gain):
    scaled = grad_out * gain
    projection = jnp.mean(scaled * values, axis=-1, keepdims=True)
    grad_in = inverse * (scaled - values * inverse * inverse * projection)
    return (grad_in, jnp.sum(grad_out * values * inverse, axis=0))


def silu_slope(values):
    sigma_v = jax.nn.sigmoid(values)
    return sigma_v * (1.0 + values * (1.0 - sigma_v))


def times(left, pieces):
    return jnp.concatenate(
        [jnp.dot(left, pieces[i], preferred_element_type=jnp.float32) for i in range(pieces.shape[0])], axis=1
    )


def against(left, pieces):
    n = pieces.shape[2]
    return sum(
        lax.dot_general(
            left[:, i * n : i * n + n], pieces[i], (((1,), (1,)), ((), ())), preferred_element_type=jnp.float32
        )
        for i in range(pieces.shape[0])
    )


def over_rows(left, right, count):
    n = right.shape[1] // count
    return jnp.stack(
        [
            lax.dot_general(
                left, right[:, i * n : i * n + n], (((0,), (0,)), ((), ())), preferred_element_type=jnp.float32
            ).astype(jnp.bfloat16)
            for i in range(count)
        ]
    )


def masked_scores(query_blk, key_blk, allowed):
    raw_scores = jnp.einsum("cid,cjd->cij", query_blk, key_blk, preferred_element_type=jnp.float32)
    return jnp.where(allowed, raw_scores, -1e30)


def body(
    tokens,
    starts,
    norm_gain,
    ema_delta,
    ema_alpha,
    ema_beta,
    ema_eta,
    ema_omega,
    mix_weight,
    value_weight,
    qk_affine,
    out_weight,
    ffn_gain,
    ffn_in,
    ffn_out,
    cotangent,
):
    seg_count, row_count, model_width = tokens.shape
    nq, ng = lax.axis_size("seq"), lax.axis_size("seg")
    grid = Grid(nq, ng)
    seq_index, seg_index = lax.axis_index("seq"), lax.axis_index("seg")
    seq_length = row_count * nq
    dims = ema_delta.shape[1]
    zdim = qk_affine.shape[0] * nq * ng // 4
    vdim = value_weight.shape[1] * ng
    token_count = seg_count * row_count
    blocks = model_width // 128

    index = seq_index * ng + seg_index
    mine = norm_gain.shape[0]
    columns = jnp.concatenate(
        [ema_delta.T, ema_alpha.T, ema_beta.T, ema_eta.T, norm_gain[None], ema_omega[None], ffn_gain[None]], axis=0
    ).astype(jnp.float32)
    count = columns.shape[0]
    tile = jnp.zeros((-(-(count + 4) // 8) * 8, 128), jnp.float32)
    tile = lax.dynamic_update_slice(tile, columns, (0, lax.rem(index * mine, 128)))
    part = qk_affine.shape[0]
    tile = lax.dynamic_update_slice(
        tile, qk_affine.astype(jnp.float32)[None], (count + index * part // 128, lax.rem(index * part, 128))
    )

    places = jnp.arange(seq_length, dtype=jnp.int32)
    goes_on = 1.0 - jnp.any(starts[0][None, :] == places[:, None], axis=1).astype(jnp.float32)
    spans = jnp.broadcast_to(jnp.min(goes_on.reshape(nq, row_count), axis=1)[:, None], (nq, 128))
    alive = lax.dynamic_slice_in_dim(goes_on, seq_index * row_count, row_count, 0)
    alive = jnp.broadcast_to(alive[:, None], (row_count, 128))

    tokens_flat = tokens.reshape(token_count, model_width).astype(jnp.float32)
    normed_b, active, x_rows, mixed_rows, carry, par, affine = mix_forward(
        grid, tokens.reshape(token_count, model_width), tile, alive, spans, dims, 0
    )
    mix_full, value_full, out_full, ffn_in_full, ffn_out_full = gather_all(
        grid, [mix_weight, value_weight, out_weight, ffn_in, ffn_out], [4, 2, 2, 4, 4], 1
    )
    gain_one = par[4 * dims].reshape(-1)
    gain_two = par[4 * dims + 2].reshape(-1)
    inverse_one = lax.rsqrt(jnp.mean(tokens_flat * tokens_flat, axis=-1, keepdims=True) + epsilon)

    projected = times(active, mix_full)
    update = jax.nn.sigmoid(projected[:, :model_width])
    gate_pre = projected[:, model_width : model_width + zdim + vdim]
    gate_rows = jax.nn.silu(gate_pre)
    shared = gate_rows[:, :zdim]
    reset_gate = gate_rows[:, zdim:]
    candidate = projected[:, model_width + zdim + vdim :]
    value_pre = times(normed_b, value_full)
    values_b = jax.nn.silu(value_pre).astype(jnp.bfloat16)
    scale_q = zdim ** (-0.5)
    query_b = (scale_q * (shared * affine[0] + affine[1])).astype(jnp.bfloat16)
    key_b = (shared * affine[2] + affine[3]).astype(jnp.bfloat16)
    positions_rows = seq_index * row_count + jnp.arange(row_count, dtype=jnp.int32)
    docs_rows = jnp.sum((starts[:, None, :] <= positions_rows[None, :, None]).astype(jnp.int32), axis=2)
    block_count = token_count // STRETCH
    block_docs = docs_rows.reshape(block_count, STRETCH)
    offsets = jnp.arange(STRETCH)
    allowed = (block_docs[:, :, None] == block_docs[:, None, :]) & (offsets[:, None] >= offsets[None, :])[None]
    query_blk = query_b.reshape(block_count, STRETCH, zdim)
    key_blk = key_b.reshape(block_count, STRETCH, zdim)
    value_blk = values_b.reshape(block_count, STRETCH, vdim)
    scores = masked_scores(query_blk, key_blk, allowed)
    row_top = jnp.max(scores, axis=2, keepdims=True)
    expo_scores = jnp.exp(scores - row_top)
    row_total = jnp.sum(expo_scores, axis=2, keepdims=True)
    probs = expo_scores / row_total
    probs_b = probs.astype(jnp.bfloat16)
    attended = jnp.einsum("cij,cjv->civ", probs_b, value_blk, preferred_element_type=jnp.float32).reshape(
        token_count, vdim
    )
    hidden_in = (attended * reset_gate).astype(jnp.bfloat16)
    hidden_pre = candidate + times(hidden_in, out_full)
    hidden_act = jax.nn.silu(hidden_pre)
    out_one = tokens_flat + update * (hidden_act - tokens_flat)
    normed_two, inverse_two = rms_forward(out_one, gain_two)
    normed_two_b = normed_two.astype(jnp.bfloat16)
    ffn_hidden = times(normed_two_b, ffn_in_full)
    ffn_act = jax.nn.silu(ffn_hidden).astype(jnp.bfloat16)
    result = (out_one + times(ffn_act, ffn_out_full)).astype(jnp.bfloat16)

    grad_y_b = cotangent.reshape(token_count, model_width)
    grad_ffn_out = over_rows(ffn_act, grad_y_b, ng)
    grad_act = against(grad_y_b, ffn_out_full)
    grad_hidden_b = (grad_act * silu_slope(ffn_hidden)).astype(jnp.bfloat16)
    grad_ffn_in = over_rows(normed_two_b, grad_hidden_b, ng)
    grad_normed_two = against(grad_hidden_b, ffn_in_full)
    grad_norm_two, grad_gain_two = rms_backward(grad_normed_two, out_one, inverse_two, gain_two)
    grad_out_one = grad_y_b.astype(jnp.float32) + grad_norm_two
    grad_update = grad_out_one * (hidden_act - tokens_flat)
    grad_tokens_flat = grad_out_one * (1.0 - update)
    grad_hpre_b = (grad_out_one * update * silu_slope(hidden_pre)).astype(jnp.bfloat16)
    grad_out_weight = over_rows(hidden_in, grad_hpre_b, ng)
    grad_hidden_in = against(grad_hpre_b, out_full)
    grad_att_b = (grad_hidden_in * reset_gate).astype(jnp.bfloat16)
    grad_reset = grad_hidden_in * attended
    grad_att_blk = grad_att_b.reshape(block_count, STRETCH, vdim)
    grad_probs = jnp.einsum("civ,cjv->cij", grad_att_blk, value_blk, preferred_element_type=jnp.float32)
    weighted = jnp.sum(probs * grad_probs, axis=2, keepdims=True)
    grad_scores_b = (probs * (grad_probs - weighted)).astype(jnp.bfloat16)
    grad_query = jnp.einsum("cij,cjd->cid", grad_scores_b, key_blk, preferred_element_type=jnp.float32).reshape(
        token_count, zdim
    )
    grad_key = jnp.einsum("cij,cid->cjd", grad_scores_b, query_blk, preferred_element_type=jnp.float32).reshape(
        token_count, zdim
    )
    grad_values = jnp.einsum("cij,civ->cjv", probs_b, grad_att_blk, preferred_element_type=jnp.float32).reshape(
        token_count, vdim
    )
    grad_qs = grad_query * scale_q
    grad_shared = grad_qs * affine[0] + grad_key * affine[2]
    grad_affine = jnp.stack(
        [
            jnp.sum(grad_qs * shared, axis=0),
            jnp.sum(grad_qs, axis=0),
            jnp.sum(grad_key * shared, axis=0),
            jnp.sum(grad_key, axis=0),
        ]
    )
    grad_gate_pre = jnp.concatenate([grad_shared, grad_reset], axis=1) * silu_slope(gate_pre)
    grad_upre = grad_update * update * (1.0 - update)
    grad_proj_b = jnp.concatenate(
        [grad_upre.astype(jnp.bfloat16), grad_gate_pre.astype(jnp.bfloat16), grad_hpre_b], axis=1
    )
    grad_mix = over_rows(active, grad_proj_b, ng)
    grad_active_b = against(grad_proj_b, mix_full).astype(jnp.bfloat16)
    grad_ema_in, m_part, k_part, omega_part = mix_backward(
        grid, grad_active_b, x_rows, mixed_rows, carry, par, alive, spans, 2
    )
    grad_vpre_b = (grad_values * silu_slope(value_pre)).astype(jnp.bfloat16)
    grad_value = over_rows(normed_b, grad_vpre_b, ng)
    grad_normed = against(grad_vpre_b, value_full) + grad_ema_in.astype(jnp.float32)
    grad_norm_one, grad_gain_one = rms_backward(grad_normed, tokens_flat, inverse_one, gain_one)
    grad_tokens = (grad_tokens_flat + grad_norm_one).astype(jnp.bfloat16)

    small = jnp.concatenate(
        [m_part, k_part, omega_part[None], grad_gain_one.reshape(1, blocks, 128), grad_gain_two.reshape(1, blocks, 128)],
        axis=0,
    ).transpose(1, 0, 2)
    if nq != blocks:
        small = jnp.take(small, np.arange(nq) * blocks // nq, axis=0)
    small = jnp.concatenate([small, jnp.broadcast_to(grad_affine[None], (nq, 4, 128))], axis=1)
    small = jnp.pad(small, ((0, 0), (0, -small.shape[1] % 8), (0, 0)))
    sums, (g_mix, g_value, g_out, g_ffn_in, g_ffn_out) = scatter_all(
        grid, small, [grad_mix, grad_value, grad_out_weight, grad_ffn_in, grad_ffn_out], [4, 2, 2, 4, 4], 3, 60 << 20
    )
    return (
        result.reshape(seg_count, row_count, model_width),
        grad_tokens.reshape(seg_count, row_count, model_width),
        *small_outputs(sums, index, dims, ema_delta, ema_alpha, ema_beta, ema_eta, mine, part, g_mix, g_value, g_out, g_ffn_in, g_ffn_out),
    )


def small_outputs(sums, index, dims, ema_delta, ema_alpha, ema_beta, ema_eta, mine, part, g_mix, g_value, g_out, g_ffn_in, g_ffn_out):
    own = lax.dynamic_slice_in_dim(sums, lax.rem(index * mine, 128), mine, 1)
    m_sum, k_sum = own[:dims].T, own[dims : 2 * dims].T
    vectors = own[2 * dims : 2 * dims + 3]
    delta, alpha, beta, eta = (v.astype(jnp.float32) for v in (ema_delta, ema_alpha, ema_beta, ema_eta))
    damping, decay = jax.nn.sigmoid(delta), jax.nn.sigmoid(alpha)
    g_keep = damping * beta * eta * k_sum
    grad_eta = damping * beta * m_sum
    grad_beta = damping * eta * m_sum
    grad_alpha = -g_keep * damping * decay * (1.0 - decay)
    grad_delta = (beta * eta * m_sum - g_keep * decay) * damping * (1.0 - damping)
    grad_affine = lax.dynamic_slice(
        sums, (2 * dims + 3 + index * part // 128, lax.rem(index * part, 128)), (1, part)
    ).reshape(-1)
    return (vectors[1], grad_delta, grad_alpha, grad_beta, grad_eta, vectors[0],
            g_mix, g_value, grad_affine, g_out, vectors[2], g_ffn_in, g_ffn_out)


def solution(mesh):
    placed = (
        P("seg", "seq", None),
        P("seg", None),
        P(("seq", "seg")),
        P(("seq", "seg"), None),
        P(("seq", "seg"), None),
        P(("seq", "seg"), None),
        P(("seq", "seg"), None),
        P(("seq", "seg")),
        P("seq", "seg"),
        P("seq", "seg"),
        P(("seq", "seg")),
        P("seq", "seg"),
        P(("seq", "seg")),
        P("seq", "seg"),
        P("seq", "seg"),
        P("seg", "seq", None),
    )
    return jax.shard_map(
        body,
        mesh=mesh,
        in_specs=placed,
        out_specs=(P("seg", "seq", None),) * 2 + placed[2:15],
        check_vma=False,
    )
```

time: 3260 us -> 598 us (0.18)
  waiting for transfers between devices: 1580 us -> 0 us
  other arithmetic: 985 us -> 43.3 us
  Pallas kernels: 0 us -> 398 us
  blocking collectives: 278 us -> 0 us
  local copies, waits for them, and re-layouts: 233 us -> 63.6 us
  matrix products: 114 us -> 79.2 us
    reduce_scatter x13 -> x0, waiting for transfers between devices: 1370 us -> none  [the longest x1 293 us: body(): lax.psum_scatter(terms[6], 'seq', scatter_dimension=0, tiled=True)]
    add_any x64 -> x0, other arithmetic: 406 us -> none  [the longest x16 242 us: advance(): jnp.einsum('ns,nsc,sch->nch', tail_mask, values, feed_pow, precision=high...]
    pallas_call x0 -> x4, Pallas kernels: none -> 398 us  [the longest x1 170 us: scatter_all(): pl.pallas_call(functools.partial(scatter_kernel, grid, shapes, count), ou...]
    all_gather x13 -> x0, blocking collectives: 216 us -> none  [the longest x1 34.4 us: body(): lax.all_gather(part_set[3], 'seq', axis=0, tiled=True)]
    dynamic_update_slice x116 -> x0, other arithmetic: 212 us -> none  [the longest x112 209 us: ema_apply(): _, outputs = lax.scan(advance, start_state, (pieces, labels, before))]
    dot_general x64 -> x0, other arithmetic: 190 us -> none  [the longest x32 156 us: advance(): jnp.einsum('isc,nis,nsc->nic', toeplitz, same_doc, values, precision=high...]
    unnamed x39 -> x0, waiting for transfers between devices: 181 us -> none
    unnamed x3 -> x0, blocking collectives: 61.6 us -> none
  transfers between devices with their start and end apart: 34 -> 0, of which waited for: 24 -> 0; matrix products, arithmetic and copies ran while one was open for 19% -> 0% of each run, Pallas kernels for 0% -> 0%
where the time goes in v1:
time: 598 us; the launch traced here: 587 us
  Pallas kernels  398 us (67%)
  matrix products  79.2 us (13%)
  local copies, waits for them, and re-layouts  63.6 us (11%)
  other arithmetic  43.3 us (7%)
    pallas_call x1, Pallas kernels, scatter_all(): pl.pallas_call(functools.partial(scatter_kernel, grid, shapes, count), ou...  170 us
    pallas_call x1, Pallas kernels, gather_all(): pl.pallas_call(functools.partial(gather_kernel, grid, shapes, count), out...  166 us
    pallas_call x1, Pallas kernels, mix_forward(): pl.pallas_call(functools.partial(mix_kernel, grid, width, dims), out_shap...  32.7 us
    dot_general x20, matrix products, against(): lax.dot_general(left[:, i * n:i * n + n], pieces[i], (((1,), (1,)), ((),...  30.8 us
    unnamed x162, local copies, waits for them, and re-layouts  30.3 us
    pallas_call x1, Pallas kernels, mix_backward(): pl.pallas_call(functools.partial(mix_back_kernel, grid, dims), out_shape=...  30.1 us
    dot_general x20, matrix products, times(): jnp.dot(left, pieces[i], preferred_element_type=jnp.float32)  24.7 us
    another operation x5, other arithmetic, over_rows(): jnp.stack([lax.dot_general(left, right[:, i * n:i * n + n], (((0,), (0,))...  16.8 us

profile of v1, /device:TPU:0, one launch (start us, length us, event | category | flops | bytes accessed | tf_op | source)
XLA Modules:
  0.0 586.7 jit_solution(16818732947645904317)
XLA Ops:
  0.6 3.5 concatenate.45
  7.8 32.7 %shard_map.271 = (bf16[256,1024]{1,0:T(8,128)(2,1)S(1)}, bf16[256,1024]{1,0:T(8,128)(2,1)S(1)}, f32[2048,128]{1,0:T(8,128)S(1)}, f32[2048,128]{1,0:T(8,128)S(1)}...) custom-call(bf16[256,1024]{1,0:T(8,128)(2,1)S(1)} %bitcast.311, ...), custom_call_target="tpu_custom_call" | custom-call | tf_op jit(solution)/shard_map/pallas_call | solution.py:550
  41.5 1.8 copy.111
  43.3 165.9 %shard_map.272 = (bf16[2,2,4,2,8,16,1056]{6,5,4,3,2,1,0:T(8,128)(2,1)}, bf16[2,2,4,2,4,32,512]{6,5,4,3,2,1,0:T(8,128)(2,1)}, bf16[2,2,4,2,4,64,256]{6,5,4,3,2,1,...) custom-call(bf16[8,16,1056]{2,1,0:T(8,128)(2,1)} %bitcast.371, ...), custom_call_target="tpu_custom_call" | custom-call | tf_op jit(solution)/shard_map/pallas_call | solution.py:195
  209.2 2.7 fusion.22
  212.9 1.1 slice.275
  214.0 2.5 copy.172
  216.5 1.8 fusion.69
  218.4 1.8 fusion.68
  221.1 1.5 multiply_convert_fusion.3
  222.7 3.4 fusion.26
  226.2 1.1 fusion.24
  227.2 1.1 fusion.20
  229.9 1.4 copy-done.8
  232.7 3.2 fusion.115
  236.0 2.9 copy.165
  238.8 2.6 multiply_convert_fusion.2
  242.8 1.2 fusion.73
  243.9 1.2 fusion.72
  245.1 1.2 fusion.71
  246.3 1.1 slice.273
  247.4 2.5 copy.171
  249.9 2.6 multiply_reduce_fusion.2
  252.6 2.7 fusion.35
  258.1 1.5 slice-done.5
  261.0 1.8 fusion.30
  262.8 1.7 fusion.28
  264.6 3.9 fusion.3
  272.5 2.1 multiply_convert_fusion.4
  276.1 1.1 copy-done.9
  277.9 2.3 fusion.125
  280.2 2.3 copy.170
  282.5 2.0 multiply_reduce_fusion.6
  285.4 1.7 copy.166
  288.9 1.1 multiply_reduce_fusion.5
  290.0 4.0 fusion.16
  294.0 2.0 copy.141
  296.0 2.0 copy.142
  298.1 1.3 pad_maximum_fusion.12
  299.4 3.0 fusion.21
  302.4 2.7 fusion.19
  305.1 2.6 fusion.46
  307.7 2.7 fusion.51.refs_0_
  310.4 30.1 %shard_map.273 = (bf16[256,1024]{1,0:T(8,128)(2,1)S(1)}, f32[16,8,128]{2,1,0:T(8,128)S(1)}, f32[16,8,128]{2,1,0:T(8,128)S(1)}, f32[8,128]{1,0:T(8,128)S(1)}) custom-call(bf16[256,1024]{1,0:T(8,128)(2,1)S(1)} %fusion.51.refs_0_, f32[2048,128]{1,0:T(8,128)S(1)} %get-tuple-element.46.refs_1_, f32[2048,128]{1,0:T(8,128)S(1)} %copy-done.3, ...), custom_call_target="tpu_custom_call" | custom-call | tf_op jit(solution)/shard_map/pallas_call | solution.py:687
  341.3 3.0 fusion.113
  344.3 3.0 fusion.18
  347.4 1.8 fusion.65
  349.2 1.8 convolution_add_fusion.8
  354.3 1.1 multiply_convert_fusion
  359.7 1.7 fusion.76
  362.2 1.8 fusion.11
  366.6 4.1 pad_maximum_fusion
  370.6 11.8 %copy.145 = bf16[4,1024,1056]{2,1,0:T(8,128)(2,1)} copy(bf16[4,1024,1056]{1,2,0:T(8,128)(2,1)} %pad_maximum_fusion) | data formatting | bytes 17301504 | tf_op jit(solution)/shard_map/stack | solution.py:746
  384.4 2.6 pad_maximum_fusion.4
  388.8 2.3 pad_maximum_fusion.5
  394.7 4.0 pad_maximum_fusion.1
  401.8 3.9 pad_maximum_fusion.2
  405.7 169.5 %shard_map.274 = (f32[8,16,1056]{2,1,0:T(8,128)}, f32[4,32,512]{2,1,0:T(8,128)}, f32[4,64,256]{2,1,0:T(8,128)}, f32[8,16,1024]{2,1,0:T(8,128)}, f32[8,64,256]{2,1,0:T(8,128)}, /*index=5*/f32[40,128]{1,0:T(8,128)}) custom-call(f32[8,40,128]{2,1,0:T(8,128)} %select_maximum_fusion.refs_0_, bf16[2,2,4,2,8,16,1056]{6,5,4,3,2,1,0:T(8,128)(2,1)} %bitcast.313, ...), custom_call_target="tpu_custom_call" | custom-call | tf_op jit(solution)/shard_map/pallas_call | solution.py:391
  575.3 1.4 dynamic-slice_bitcast_fusion.2
  576.7 1.4 subtract_multiply_fusion
  578.1 2.1 copy.146
  580.2 1.3 dynamic-slice_bitcast_fusion.5
  581.4 1.7 copy.179
  583.1 1.7 copy.180
  (234 shorter events, 47.2 us)
Async XLA Ops:
  216.5 3.7 copy-start.40
  218.3 2.8 copy-start.44
  220.7 2.0 copy-start.46
  220.7 5.5 copy-start.58
  221.1 5.0 copy-start.47
  226.2 2.2 copy-start.30
  227.2 2.2 copy-start.31
  227.2 1.6 copy-start.22
  228.9 2.9 copy-start.70
  231.6 7.3 %copy-start.54 = (bf16[256,128]{1,0:T(8,128)(2,1)}, bf16[256,128]{1,0:T(8,128)(2,1)S(1)}, u32[]{:S(2)}) copy-start(bf16[256,128]{1,0:T(8,128)(2,1)S(1)} %copy.168) | copy-start | bytes 196612
  231.7 7.1 %copy-start.56 = (bf16[256,128]{1,0:T(8,128)(2,1)}, bf16[256,128]{1,0:T(8,128)(2,1)S(1)}, u32[]{:S(2)}) copy-start(bf16[256,128]{1,0:T(8,128)(2,1)S(1)} %copy.169) | copy-start | bytes 196612
  238.8 3.5 copy-start.15
  241.4 3.7 copy-start.6
  243.9 2.4 copy-start.24
  246.3 3.6 copy-start.1
  249.9 2.6 copy-start.34
  249.9 5.4 slice-start
  252.5 19.3 %copy-start.13 = (f32[256,1024]{1,0:T(8,128)}, f32[256,1024]{1,0:T(8,128)S(1)}, u32[]{:S(2)}) copy-start(f32[256,1024]{1,0:T(8,128)S(1)} %get-tuple-element.111) | copy-start | bytes 3145732
  252.6 3.3 slice-start.1
  255.9 2.2 slice-start.4
  256.6 2.9 slice-start.5
  259.5 3.3 copy-start.19
  260.3 4.3 copy-start.48
  261.0 3.5 copy-start.50
  268.5 2.3 copy-start.28
  270.7 1.5 copy-start.25
  270.8 1.6 copy-start.37
  270.8 1.6 copy-start.38
  270.8 1.7 copy-start.39
  271.8 2.8 copy-start.32
  272.5 2.2 copy-start.16
  275.6 1.6 copy-start.9
  275.6 2.3 copy-start.10
  277.9 4.6 copy-start.64
  280.2 4.4 copy-start.57
  280.2 6.9 %copy-start.55 = (bf16[256,128]{1,0:T(8,128)(2,1)S(1)}, bf16[256,128]{1,0:T(8,128)(2,1)}, u32[]{:S(2)}) copy-start(bf16[256,128]{1,0:T(8,128)(2,1)} %copy-done.54) | copy-start | bytes 196612
  282.5 2.0 copy-start.65
  299.4 3.0 copy-start.61
  299.4 3.0 copy-start.59
  302.4 2.7 copy-start.17
  307.7 2.7 copy-start.3
  344.3 11.1 %slice-start.2 = ((s8[8388608]{0:T(1024)(128)(4,1)}), s8[4194304]{0:T(1024)(128)(4,1)S(1)}, s32[]{:S(2)}) async-start(s8[8388608]{0:T(1024)(128)(4,1)} %bitcast.333), calls=%async_computation.2 | async-start | bytes 8388608
  347.4 3.7 copy-start.41
  349.2 3.6 copy-start.53
  351.0 4.4 slice-start.3
  352.1 1.6 copy-start.49
  352.1 1.9 copy-start.51
  352.1 2.2 copy-start.52
  355.5 2.3 copy-start.42
  357.8 1.8 copy-start.33
  357.8 2.0 copy-start.35
  361.6 2.5 copy-start.18
  384.3 2.6 copy-start.7
  384.4 2.6 copy-start.27
  388.7 2.3 copy-start.20
  388.7 2.9 copy-start.29
  394.7 4.0 copy-start.36
  394.7 4.0 copy-start.43
  405.7 171.0 %copy-start.66 = (bf16[32,16]{0,1:T(8,128)(2,1)S(1)}, bf16[32,16]{0,1:T(8,128)(2,1)}, u32[]{:S(2)}) copy-start(bf16[32,16]{0,1:T(8,128)(2,1)} %param.19) | copy-start | bytes 3076
  405.7 171.0 %copy-start.67 = (bf16[32,16]{0,1:T(8,128)(2,1)S(1)}, bf16[32,16]{0,1:T(8,128)(2,1)}, u32[]{:S(2)}) copy-start(bf16[32,16]{0,1:T(8,128)(2,1)} %param.20) | copy-start | bytes 3076
  405.7 171.0 %copy-start.68 = (bf16[32,16]{0,1:T(8,128)(2,1)S(1)}, bf16[32,16]{0,1:T(8,128)(2,1)}, u32[]{:S(2)}) copy-start(bf16[32,16]{0,1:T(8,128)(2,1)} %param.21) | copy-start | bytes 3076
  405.7 171.0 %copy-start.69 = (bf16[32,16]{0,1:T(8,128)(2,1)S(1)}, bf16[32,16]{0,1:T(8,128)(2,1)}, u32[]{:S(2)}) copy-start(bf16[32,16]{0,1:T(8,128)(2,1)} %param.22) | copy-start | bytes 3076
  575.2 9.5 %copy-start.63 = (f32[8,16,1024]{2,1,0:T(8,128)S(1)}, f32[8,16,1024]{2,1,0:T(8,128)}, u32[]{:S(2)}) copy-start(f32[8,16,1024]{2,1,0:T(8,128)} %get-tuple-element.57) | copy-start | bytes 1572868
  575.2 10.3 %copy-start.62 = (f32[8,64,256]{2,1,0:T(8,128)S(1)}, f32[8,64,256]{2,1,0:T(8,128)}, u32[]{:S(2)}) copy-start(f32[8,64,256]{2,1,0:T(8,128)} %get-tuple-element.58) | copy-start | bytes 1572868
  (13 other events, 14.8 us)

commit v2 on v1

--- a/solution.py
+++ b/solution.py
@@ -11,6 +11,8 @@
 
 STRETCH = 128
 epsilon = 1e-05
+GATHER_CUTS = (4, 4, 4, 4, 8)
+SCATTER_CUTS = (4, 4, 2, 4, 2)
 
 MESH = pl.DeviceIdType.MESH
 ANY = pl.BlockSpec(memory_space=pl.ANY)
@@ -68,153 +70,136 @@
         return self.send.at[i], self.recv.at[i]
 
 
-def gather_kernel(grid, shapes, count, *refs):
+def gather_steps(grid, shapes, shards, wholes, own_sem, sems):
     n = len(shapes)
-    shards, wholes = refs[:n], refs[n : 2 * n]
-    own_sem, send, recv = refs[2 * n :]
-    sems = Sems(send, recv)
     z, x, y, c = grid.here()
-    enter(grid, grid.peers("zxyc"))
     pending = []
 
     def push(src, dst, axis, d, arrives):
         s, r = sems.take()
-        copy = pltpu.make_async_remote_copy(
-            src, dst, s, r, device_id=grid.device(grid.peer(axis, d)), device_id_type=MESH
-        )
+        device = grid.device(grid.peer(axis, d))
+        copy = pltpu.make_async_remote_copy(src, dst, s, r, device_id=device, device_id_type=MESH)
         copy.start()
         pending.append(copy)
-        there = pltpu.make_async_remote_copy(
-            arrives, arrives, s, r, device_id=grid.device(grid.peer(axis, d)), device_id_type=MESH
+        there = pltpu.make_async_remote_copy(arrives, arrives, s, r, device_id=device, device_id_type=MESH)
+        return there.wait_recv
+
+    def back(axis, d):
+        return dict(zip("zxyc", grid.peer(axis, grid.size(axis) - d)))[axis]
+
+    owns = []
+    chunks = [(i, q) for i in range(n) for q in range(shapes[i][0] // 2)]
+    core_waits = {}
+
+    def core(k, view):
+        core_waits.setdefault(k, []).extend(
+            push(view(c), view(c), "c", d, view(back("c", d))) for d in range(1, grid.nc)
         )
-        return there.wait_recv
-
-    def back(axis, d):
-        place = grid.peer(axis, grid.size(axis) - d)
-        return dict(zip("zxyc", place))
-
-    owns = []
-    for i in range(n):
-        copy = pltpu.make_async_copy(shards[i], wholes[i].at[y, c, z, x], own_sem.at[i])
-        copy.start()
-        owns.append(copy)
-
-    chunks = [(i, q) for i in range(n) for q in range(shapes[i][0] // 2)]
-    halves = (0, 1)
-    core_waits = []
-
-    def core(view):
-        core_waits.extend(
-            push(view(c), view(c), "c", d, view(back("c", d)["c"])) for d in range(1, grid.nc)
-        )
-
-    def stage_z(i, h):
+
+    def stage_z(k, i, h):
         w = wholes[i]
         return [
-            push(shards[i].at[h], w.at[y, c, z, x, h], "z", d, w.at[y, c, back("z", d)["z"], x, h])
+            push(shards[i].at[h], w.at[y, c, z, x, h], "z", d, w.at[y, c, back("z", d), x, h])
             for d in range(1, grid.nz)
         ]
 
-    def stage_two(i, h):
+    def stage_two(k, i, h):
         w = wholes[i]
-        core(lambda cc: w.at[y, cc, :, x, h])
         src = w.at[y, c, :, x, h]
         if h % 2 == 0:
-            return [push(src, src, "x", d, w.at[y, c, :, back("x", d)["x"], h]) for d in range(1, grid.nx)]
-        return [push(src, src, "y", d, w.at[back("y", d)["y"], c, :, x, h]) for d in range(1, grid.ny)]
-
-    def stage_three(i, h):
+            waits = [push(src, src, "x", d, w.at[y, c, :, back("x", d), h]) for d in range(1, grid.nx)]
+        else:
+            waits = [push(src, src, "y", d, w.at[back("y", d), c, :, x, h]) for d in range(1, grid.ny)]
+        core(k, lambda cc: w.at[y, cc, :, x, h])
+        return waits
+
+    def stage_three(k, i, h):
         w = wholes[i]
         if h % 2 == 0:
+            src = w.at[y, c, :, :, h]
+            waits = [push(src, src, "y", d, w.at[back("y", d), c, :, :, h]) for d in range(1, grid.ny)]
             for d in range(1, grid.nx):
-                core(lambda cc: w.at[y, cc, :, back("x", d)["x"], h])
-            src = w.at[y, c, :, :, h]
-            return [push(src, src, "y", d, w.at[back("y", d)["y"], c, :, :, h]) for d in range(1, grid.ny)]
+                core(k, lambda cc: w.at[y, cc, :, back("x", d), h])
+            return waits
+        src = w.at[:, c, :, x, h]
+        waits = [push(src, src, "x", d, w.at[:, c, :, back("x", d), h]) for d in range(1, grid.nx)]
         for d in range(1, grid.ny):
-            core(lambda cc: w.at[back("y", d)["y"], cc, :, x, h])
-        src = w.at[:, c, :, x, h]
-        return [push(src, src, "x", d, w.at[:, c, :, back("x", d)["x"], h]) for d in range(1, grid.nx)]
-
-    def stage_last(i, h):
+            core(k, lambda cc: w.at[back("y", d), cc, :, x, h])
+        return waits
+
+    def stage_last(k, i, h):
         w = wholes[i]
         if h % 2 == 0:
             for d in range(1, grid.ny):
-                core(lambda cc: w.at[back("y", d)["y"], cc, :, :, h])
+                core(k, lambda cc: w.at[back("y", d), cc, :, :, h])
         else:
             for d in range(1, grid.nx):
-                core(lambda cc: w.at[:, cc, :, back("x", d)["x"], h])
+                core(k, lambda cc: w.at[:, cc, :, back("x", d), h])
 
     def finish(waits):
         for wait in waits:
             wait()
 
-    got_z, got_two, got_three = {}, {}, {}
-    ahead = 2
+    got = {}
     total = len(chunks)
-    for t in range(total + 3 + ahead):
-        k = t
-        if k < total:
-            i, q = chunks[k]
-            for h in halves:
-                got_z[k, h] = stage_z(i, 2 * q + h)
-        k = t - ahead
+    for t in range(-1, total + 3):
+        if t == 0:
+            for i in range(n):
+                copy = pltpu.make_async_copy(shards[i], wholes[i].at[y, c, z, x], own_sem.at[i])
+                copy.start()
+                owns.append(copy)
+        if 0 <= t < total:
+            i, q = chunks[t]
+            if q == 0:
+                owns[i].wait()
+            for h in (0, 1):
+                finish(got[t, h])
+                got[t, h] = stage_two(t, i, 2 * q + h)
+        if t + 1 < total:
+            i, q = chunks[t + 1]
+            for h in (0, 1):
+                got[t + 1, h] = stage_z(t + 1, i, 2 * q + h)
+        k = t - 1
         if 0 <= k < total:
             i, q = chunks[k]
-            if q == 0:
-                owns[i].wait()
-            for h in halves:
-                finish(got_z[k, h])
-                got_two[k, h] = stage_two(i, 2 * q + h)
-        k = t - ahead - 1
+            for h in (0, 1):
+                finish(got[k, h])
+                got[k, h] = stage_three(k, i, 2 * q + h)
+        k = t - 2
         if 0 <= k < total:
             i, q = chunks[k]
-            for h in halves:
-                finish(got_two[k, h])
-                got_three[k, h] = stage_three(i, 2 * q + h)
-        k = t - ahead - 2
+            for h in (0, 1):
+                finish(got[k, h])
+                stage_last(k, i, 2 * q + h)
+        k = t - 3
+        done = []
         if 0 <= k < total:
+            finish(core_waits[k])
             i, q = chunks[k]
-            for h in halves:
-                finish(got_three[k, h])
-                stage_last(i, 2 * q + h)
-    finish(core_waits)
-    for copy in pending:
-        copy.wait_send()
-    assert sems.used <= count, sems.used
-
-
-def gather_all(grid, shards, cuts, collective_id):
+            if q + 1 == shapes[i][0] // 2:
+                done = [i]
+        if t == total + 2:
+            for copy in pending:
+                copy.wait_send()
+        yield done
+
+
+def gather_plan(grid, shards, cuts):
     shapes, args, outs = [], [], []
     for w, q in zip(shards, cuts):
         k, n = w.shape
+        q = max(1, min(q, k // 32))
         shapes.append((2 * q, k // (2 * q), n))
         args.append(w.reshape(shapes[-1]))
         outs.append(jax.ShapeDtypeStruct((grid.ny, grid.nc, grid.nz, grid.nx) + shapes[-1], w.dtype))
     per = (grid.nz - 1) + (grid.nx - 1) + (grid.ny - 1) + (grid.nc - 1) * (grid.nx + grid.ny)
     count = sum(s[0] for s in shapes) * per
-    wholes = pl.pallas_call(
-        functools.partial(gather_kernel, grid, shapes, count),
-        out_shape=outs,
-        in_specs=[ANY] * len(args),
-        out_specs=[ANY] * len(args),
-        scratch_shapes=[
-            pltpu.SemaphoreType.DMA((len(args),)),
-            pltpu.SemaphoreType.DMA((count,)),
-            pltpu.SemaphoreType.DMA((count,)),
-        ],
-        compiler_params=pltpu.CompilerParams(collective_id=collective_id, has_side_effects=True),
-    )(*args)
-    return [w.reshape(grid.ng, -1, w.shape[-1]) for w in wholes]
-
-
-def scatter_kernel(grid, shapes, count, *refs):
+    return shapes, args, outs, count
+
+
+def scatter_steps(grid, shapes, terms, sums, scratch, own_sem, sems):
     n = len(shapes)
     nz, nx, ny, nc = grid.nz, grid.nx, grid.ny, grid.nc
-    nq, ng = grid.nq, grid.ng
-    small, refs = refs[0], refs[1:]
-    terms, sums = refs[:n], refs[n : 2 * n]
-    small_sum, small_seq, small_seg, s_send, s_recv = refs[2 * n : 2 * n + 5]
-    scratch = refs[2 * n + 5 :]
     own = [scratch[7 * i] for i in range(n)]
     one = [scratch[7 * i + 1] for i in range(n)]
     two_a = [scratch[7 * i + 2] for i in range(n)]
@@ -222,45 +207,8 @@
     three_a = [scratch[7 * i + 4] for i in range(n)]
     three_b = [scratch[7 * i + 5] for i in range(n)]
     four = [scratch[7 * i + 6] for i in range(n)]
-    own_sem, send, recv = scratch[7 * n :]
-    sems = Sems(send, recv)
     z, x, y, c = grid.here()
-    sq, sg = lax.axis_index("seq"), lax.axis_index("seg")
-    seq_peer = [{"seq": lax.rem(sq + d, nq), "seg": sg} for d in range(1, nq)]
-    seg_peer = [{"seq": sq, "seg": lax.rem(sg + d, ng)} for d in range(1, ng)]
-    barrier = pltpu.get_barrier_semaphore()
-    for place in seq_peer + seg_peer:
-        pl.semaphore_signal(barrier, inc=1, device_id=place, device_id_type=MESH)
-    pl.semaphore_wait(barrier, nq + ng - 2)
     pending = []
-
-    small_copies = []
-    for d in range(1, nq):
-        small_copies.append(pltpu.make_async_remote_copy(
-            small.at[lax.rem(sq + d, nq)], small_seq.at[d - 1], s_send.at[d - 1], s_recv.at[d - 1],
-            device_id=seq_peer[d - 1], device_id_type=MESH))
-        small_copies[-1].start()
-
-    def small_middle():
-        total = small[sq]
-        for d in range(1, nq):
-            small_copies[d - 1].wait_recv()
-            total += small_seq[d - 1]
-        small_sum[...] = total
-        for d in range(1, ng):
-            small_copies.append(pltpu.make_async_remote_copy(
-                small_sum, small_seg.at[d - 1], s_send.at[nq + d - 2], s_recv.at[nq + d - 2],
-                device_id=seg_peer[d - 1], device_id_type=MESH))
-            small_copies[-1].start()
-
-    def small_end():
-        total = small_sum[...]
-        for d in range(1, ng):
-            small_copies[nq + d - 2].wait_recv()
-            total += small_seg[d - 1]
-        for copy in small_copies:
-            copy.wait_send()
-        small_sum[...] = total
 
     def push(src, dst, axis, d):
         s, r = sems.take()
@@ -348,8 +296,6 @@
     chunks = [(i, q) for i in range(n) for q in range(shapes[i][0] // 2)]
     waits = {}
     for t in range(len(chunks) + len(stages) - 1):
-        if t == 1:
-            small_middle()
         for j, stage in enumerate(stages):
             if 0 <= t - j < len(chunks):
                 i, q = chunks[t - j]
@@ -361,20 +307,81 @@
                 i, q = chunks[t]
                 for h in (0, 1):
                     waits[i, q, h] += load_own(i, q, h)
-    small_end()
-    for copy in pending:
-        copy.wait_send()
-    assert sems.used <= count, sems.used
-
-
-def scatter_all(grid, small, terms, cuts, collective_id, vmem):
-    nz, nx, ny, nc = grid.nz, grid.nx, grid.ny, grid.nc
+        if t == len(chunks) + len(stages) - 2:
+            for copy in pending:
+                copy.wait_send()
+        yield
+
+
+class SmallSum:
+    def __init__(self, grid, small, total, seq_in, seg_in, send, recv):
+        self.grid, self.small, self.total = grid, small, total
+        self.seq_in, self.seg_in, self.send, self.recv = seq_in, seg_in, send, recv
+        self.seq_peer, self.seg_peer = small_peers(grid)
+        self.copies = []
+
+    def push(self, src, dst, device):
+        i = len(self.copies)
+        copy = pltpu.make_async_remote_copy(
+            src, dst, self.send.at[i], self.recv.at[i], device_id=device, device_id_type=MESH
+        )
+        copy.start()
+        self.copies.append(copy)
+
+    def start(self):
+        nq, sq = self.grid.nq, lax.axis_index("seq")
+        for d in range(1, nq):
+            self.push(self.small.at[lax.rem(sq + d, nq)], self.seq_in.at[d - 1], self.seq_peer[d - 1])
+
+    def middle(self):
+        nq, ng = self.grid.nq, self.grid.ng
+        total = self.small[lax.axis_index("seq")]
+        for d in range(1, nq):
+            self.copies[d - 1].wait_recv()
+            total += self.seq_in[d - 1]
+        self.total[...] = total
+        for d in range(1, ng):
+            self.push(self.total, self.seg_in.at[d - 1], self.seg_peer[d - 1])
+
+    def end(self):
+        nq, ng = self.grid.nq, self.grid.ng
+        total = self.total[...]
+        for d in range(1, ng):
+            self.copies[nq + d - 2].wait_recv()
+            total += self.seg_in[d - 1]
+        for copy in self.copies:
+            copy.wait_send()
+        self.total[...] = total
+
+
+def small_peers(grid):
+    nq, ng = grid.nq, grid.ng
+    s, g = lax.axis_index("seq"), lax.axis_index("seg")
+    return (
+        [{"seq": lax.rem(s + d, nq), "seg": g} for d in range(1, nq)],
+        [{"seq": s, "seg": lax.rem(g + d, ng)} for d in range(1, ng)],
+    )
+
+
+def meet(peers):
+    barrier = pltpu.get_barrier_semaphore()
+    for place in peers:
+        pl.semaphore_signal(barrier, inc=1, device_id=place, device_id_type=MESH)
+    pl.semaphore_wait(barrier, len(peers))
+
+
+def scatter_plan(grid, terms, cuts):
+    nz, nx, ny = grid.nz, grid.nx, grid.ny
     shapes, args, outs, scratch = [], [], [], []
     for t, q in zip(terms, cuts):
         _, rows, n = t.shape
-        kh = rows // grid.nq // (2 * q)
+        if n < 128:
+            rows, n = rows * n // 128, 128
+        k = rows // grid.nq
+        q = max(1, min(q, k // 32))
+        kh = k // (2 * q)
         shapes.append((2 * q, kh, n))
-        args.append(t.reshape(ny, nc, nz, nx, 2 * q, kh, n))
+        args.append(t.reshape(ny, grid.nc, nz, nx, 2 * q, kh, n))
         outs.append(jax.ShapeDtypeStruct((2 * q, kh, n), jnp.float32))
         b = t.dtype
         scratch += [
@@ -386,49 +393,38 @@
             pltpu.VMEM((q, max(ny - 1, 1), nz, kh, n), b),
             pltpu.VMEM((q, 2, max(nz - 1, 1), kh, n), b),
         ]
-    per = (nc - 1) + (nx - 1) + (ny - 1) + (nz - 1)
+    per = (grid.nc - 1) + (nx - 1) + (ny - 1) + (nz - 1)
     count = per * sum(s[0] for s in shapes)
-    sums = pl.pallas_call(
-        functools.partial(scatter_kernel, grid, shapes, count),
-        out_shape=outs + [jax.ShapeDtypeStruct(small.shape[1:], small.dtype)],
-        in_specs=[pl.BlockSpec(memory_space=pltpu.VMEM)] + [ANY] * len(args),
-        out_specs=[pl.BlockSpec(memory_space=pltpu.VMEM)] * (len(args) + 1),
-        scratch_shapes=[
-            pltpu.VMEM((grid.nq - 1,) + small.shape[1:], small.dtype),
-            pltpu.VMEM((grid.ng - 1,) + small.shape[1:], small.dtype),
-            pltpu.SemaphoreType.DMA((grid.nq + grid.ng - 2,)),
-            pltpu.SemaphoreType.DMA((grid.nq + grid.ng - 2,)),
-        ]
-        + scratch
-        + [
-            pltpu.SemaphoreType.DMA((len(args), 2)),
-            pltpu.SemaphoreType.DMA((count,)),
-            pltpu.SemaphoreType.DMA((count,)),
-        ],
-        compiler_params=pltpu.CompilerParams(
-            collective_id=collective_id, has_side_effects=True, vmem_limit_bytes=vmem
-        ),
-    )(small, *args)
-    return sums[-1], [s.reshape(-1, s.shape[-1]) for s in sums[:-1]]
+    return shapes, args, outs, scratch, count
 
 
 def block_of(e, nq, blocks):
     return e * blocks // nq
 
 
-def mix_kernel(grid, width, dims, *refs):
-    (tok, tile, alive, spans, normed_out, active_out, x_out, mixed_out, carry_out, par_out, aff_out,
-     tiles, table, bound, sends_t, recv_t, sends_b, recv_b) = refs
+def mix_kernel(grid, width, dims, shapes, *refs):
+    n = len(shapes)
+    shards, refs = refs[:n], refs[n:]
+    tok, tile, alive, spans, mask, *refs = refs
+    wholes, refs = refs[:n], refs[n:]
+    (normed_out, active_out, x_out, mixed_out, carry_out, par_out, aff_out, probs_out, out_one_out, two_out, layer_out,
+     proj_hbm, value_hbm, att_hbm, hin_hbm, hpre_hbm, ffn_hbm, act_hbm,
+     proj, value_pre, att, hin, hpre, ffn_pre, act, values,
+     tiles, table, bound, sends_t, recv_t, sends_b, recv_b, own_sem, flush_sem, load_sem, send, recv,
+     *slots) = refs
     nq, ng = grid.nq, grid.ng
     rows = tok.shape[0]
     blocks = width // 128
-    s, g = lax.axis_index("seq"), lax.axis_index("seg")
-    seq_peer = [{"seq": lax.rem(s + d, nq), "seg": g} for d in range(1, nq)]
-    seg_peer = [{"seq": s, "seg": lax.rem(g + d, ng)} for d in range(1, ng)]
-    barrier = pltpu.get_barrier_semaphore()
-    for place in seq_peer + seg_peer:
-        pl.semaphore_signal(barrier, inc=1, device_id=place, device_id_type=MESH)
-    pl.semaphore_wait(barrier, nq + ng - 2)
+    s = lax.axis_index("seq")
+    seq_peer, seg_peer = small_peers(grid)
+    meet(seq_peer + seg_peer)
+    steps = gather_steps(grid, shapes, shards, wholes, own_sem, Sems(send, recv))
+
+    done = set()
+
+    def pump(count=1):
+        for _ in range(count):
+            done.update(next(steps, ()))
 
     copies = []
     for d in range(1, ng):
@@ -436,6 +432,7 @@
             tile, tiles.at[d - 1], sends_t.at[d - 1], recv_t.at[d - 1],
             device_id=seg_peer[d - 1], device_id_type=MESH))
         copies[-1].start()
+    pump()
     for copy in copies:
         copy.wait_recv()
     lanes = tile[...]
@@ -464,6 +461,8 @@
         aff += table[e, count : count + 4]
     aff_out[...] = aff
 
+    pump()
+
     gain = [par_out[4 * dims, b : b + 1, :] for b in range(blocks)]
     step_rows = 32
 
@@ -500,6 +499,7 @@
             bound.at[s], bound.at[s], sends_b.at[d - 1], recv_b.at[d - 1],
             device_id=seq_peer[d - 1], device_id_type=MESH))
         out[-1].start()
+    pump()
     for d in range(1, nq):
         came = bound.at[lax.rem(s + nq - d, nq)]
         pltpu.make_async_remote_copy(
@@ -522,12 +522,120 @@
         mixed_out[pl.ds(pl.multiple_of(p * blocks, blocks), blocks), :] = sums[0]
         return state
 
-    lax.fori_loop(0, rows, second_pass, tuple(carry_out[j] for j in range(dims)), unroll=4)
+    state = tuple(carry_out[j] for j in range(dims))
+    for half in range(2):
+        state = lax.fori_loop(half * rows // 2, (half + 1) * rows // 2, second_pass, state, unroll=4)
+        pump()
     for b in range(blocks):
         m = mixed_out[pl.ds(b, rows, stride=blocks), :]
         active_out[:, b * 128 : b * 128 + 128] = (m * jax.nn.sigmoid(m)).astype(jnp.bfloat16)
     for copy in copies + out:
         copy.wait_send()
+
+    flushes = []
+
+    def flush(ref, hbm):
+        copy = pltpu.make_async_copy(ref, hbm, flush_sem.at[len(flushes)])
+        copy.start()
+        flushes.append(copy)
+
+    def pieces(i):
+        while i not in done:
+            pump()
+
+        def fetch(g):
+            return pltpu.make_async_copy(
+                wholes[i].at[g // grid.nc, g % grid.nc], slots[i].at[g % 2], load_sem.at[i, g % 2]
+            )
+
+        fetch(0).start()
+        for g in range(grid.ng):
+            if g + 1 < grid.ng:
+                fetch(g + 1).start()
+            fetch(g).wait()
+            piece = slots[i][g % 2]
+            wide = piece.shape[-1]
+            yield g, slice(g * wide, g * wide + wide), piece.reshape(-1, wide)
+            if g % 2:
+                pump()
+
+    block_rows = 32
+    zdim = aff_out.shape[1]
+    vdim = value_pre.shape[1]
+    first_gate, first_reset, first_cand = width, width + zdim, width + zdim + vdim
+    dot = functools.partial(jnp.dot, preferred_element_type=jnp.float32)
+
+    def by_rows(count=rows, each=block_rows):
+        def wrap(f):
+            pl.loop(0, count // each)(lambda i: f(pl.ds(pl.multiple_of(i * each, each), each)))
+
+        return wrap
+
+    for g, cols, piece in pieces(0):
+        proj[:, cols] = dot(active_out[...], piece)
+    flush(proj, proj_hbm)
+
+    scale_q = zdim**-0.5
+    near = []
+    for r in range(rows // STRETCH):
+        at = slice(r * STRETCH, r * STRETCH + STRETCH)
+        gate = proj[at, first_gate:first_reset]
+        shared = gate * jax.nn.sigmoid(gate)
+        query = (scale_q * (shared * aff_out[0:1] + aff_out[1:2])).astype(jnp.bfloat16)
+        key = (shared * aff_out[2:3] + aff_out[3:4]).astype(jnp.bfloat16)
+        scores = lax.dot_general(query, key, (((1,), (1,)), ((), ())), preferred_element_type=jnp.float32)
+        scores = jnp.where(mask[at, :] > 0.0, scores, -1e30)
+        expo = jnp.exp(scores - jnp.max(scores, axis=1, keepdims=True))
+        probs = expo / jnp.sum(expo, axis=1, keepdims=True)
+        probs_out[at, :] = probs
+        near.append(probs.astype(jnp.bfloat16))
+
+    for g, cols, piece in pieces(1):
+        pre = dot(normed_out[...], piece)
+        value_pre[:, cols] = pre
+        values[:, cols] = (pre * jax.nn.sigmoid(pre)).astype(jnp.bfloat16)
+    flush(value_pre, value_hbm)
+    for r in range(rows // STRETCH):
+        at = slice(r * STRETCH, r * STRETCH + STRETCH)
+        att[at, :] = dot(near[r], values[at, :])
+
+    @by_rows()
+    def _(at):
+        gate = proj[at, first_reset:first_cand]
+        hin[at, :] = (att[at, :] * (gate * jax.nn.sigmoid(gate))).astype(jnp.bfloat16)
+
+    flush(att, att_hbm)
+    flush(hin, hin_hbm)
+
+    for g, cols, piece in pieces(2):
+        hpre[:, cols] = proj[:, first_cand + cols.start : first_cand + cols.stop] + dot(hin[...], piece)
+    flush(hpre, hpre_hbm)
+
+    gain_two = [par_out[4 * dims + 2, b : b + 1, :] for b in range(blocks)]
+
+    @by_rows()
+    def _(at):
+        v = tok[at, :].astype(jnp.float32)
+        h = hpre[at, :]
+        one = v + jax.nn.sigmoid(proj[at, 0:width]) * (h * jax.nn.sigmoid(h) - v)
+        out_one_out[at, :] = one
+        r = lax.rsqrt(jnp.mean(one * one, axis=1, keepdims=True) + epsilon)
+        for b in range(blocks):
+            lane = slice(b * 128, b * 128 + 128)
+            two_out[at, lane] = (one[:, lane] * r * gain_two[b]).astype(jnp.bfloat16)
+
+    for g, cols, piece in pieces(3):
+        pre = dot(two_out[...], piece)
+        ffn_pre[:, cols] = pre
+        act[:, cols] = (pre * jax.nn.sigmoid(pre)).astype(jnp.bfloat16)
+    flush(ffn_pre, ffn_hbm)
+    flush(act, act_hbm)
+    for g, cols, piece in pieces(4):
+        layer_out[:, cols] = (out_one_out[:, cols] + dot(act[...], piece)).astype(jnp.bfloat16)
+    for _ in steps:
+        pass
+    for copy in flushes:
+        copy.wait()
 
 
 def power(v, n):
@@ -541,26 +649,46 @@
     return result
 
 
-def mix_forward(grid, tok, tile, alive, spans, dims, collective_id):
+def mix_forward(grid, weights, cuts, tok, tile, alive, spans, mask, dims, collective_id):
     rows, width = tok.shape
     nq, ng = grid.nq, grid.ng
     blocks = width // 128
     f = jnp.float32
     vm = pl.BlockSpec(memory_space=pltpu.VMEM)
-    return pl.pallas_call(
-        functools.partial(mix_kernel, grid, width, dims),
-        out_shape=[
-            jax.ShapeDtypeStruct((rows, width), jnp.bfloat16),
-            jax.ShapeDtypeStruct((rows, width), jnp.bfloat16),
-            jax.ShapeDtypeStruct((rows * blocks, 128), f),
-            jax.ShapeDtypeStruct((rows * blocks, 128), f),
-            jax.ShapeDtypeStruct((dims, blocks, 128), f),
-            jax.ShapeDtypeStruct((4 * dims + 3, blocks, 128), f),
-            jax.ShapeDtypeStruct((4, 128), f),
-        ],
-        in_specs=[vm] * 4,
-        out_specs=[vm] * 7,
-        scratch_shapes=[
+    shapes, shards, outs, count = gather_plan(grid, weights, cuts)
+    n = len(shards)
+    vdim, fdim, proj_dim = weights[1].shape[1] * ng, weights[3].shape[1] * ng, weights[0].shape[1] * ng
+    low = jnp.bfloat16
+    kept = [
+        ((rows, proj_dim), f),
+        ((rows, vdim), f),
+        ((rows, vdim), f),
+        ((rows, vdim), low),
+        ((rows, width), f),
+        ((rows, fdim), f),
+        ((rows, fdim), low),
+    ]
+    local = [
+        ((rows, width), low),
+        ((rows, width), low),
+        ((rows * blocks, 128), f),
+        ((rows * blocks, 128), f),
+        ((dims, blocks, 128), f),
+        ((4 * dims + 3, blocks, 128), f),
+        ((4, 128), f),
+        ((rows, STRETCH), f),
+        ((rows, width), f),
+        ((rows, width), low),
+        ((rows, width), low),
+    ]
+    result = pl.pallas_call(
+        functools.partial(mix_kernel, grid, width, dims, shapes),
+        out_shape=outs + [jax.ShapeDtypeStruct(*v) for v in local + kept],
+        in_specs=[ANY] * n + [vm] * 5,
+        out_specs=[ANY] * n + [vm] * len(local) + [ANY] * len(kept),
+        scratch_shapes=[pltpu.VMEM(*v) for v in kept]
+        + [
+            pltpu.VMEM((rows, vdim), low),
             pltpu.VMEM((ng - 1,) + tile.shape, f),
             pltpu.VMEM((nq,) + tile.shape, f),
             pltpu.VMEM((nq, dims, blocks, 128), f),
@@ -568,25 +696,42 @@
             pltpu.SemaphoreType.DMA((nq + ng - 2,)),
             pltpu.SemaphoreType.DMA((nq - 1,)),
             pltpu.SemaphoreType.DMA((nq - 1,)),
-        ],
+            pltpu.SemaphoreType.DMA((n,)),
+            pltpu.SemaphoreType.DMA((len(kept),)),
+            pltpu.SemaphoreType.DMA((n, 2)),
+            pltpu.SemaphoreType.DMA((count,)),
+            pltpu.SemaphoreType.DMA((count,)),
+        ]
+        + [pltpu.VMEM((2,) + o.shape[2:], o.dtype) for o in outs],
         compiler_params=pltpu.CompilerParams(
-            collective_id=collective_id, has_side_effects=True, vmem_limit_bytes=40 << 20
+            collective_id=collective_id, has_side_effects=True, vmem_limit_bytes=60 << 20
         ),
-    )(tok, tile, alive, spans)
-
-
-def mix_back_kernel(grid, dims, *refs):
-    (gact, x_in, mixed, carry, par, alive, spans, gin_out, m_out, k_out, om_out,
-     g_rows, gin_rows, before, bound, sends_b, recv_b) = refs
+    )(*shards, tok, tile, alive, spans, mask)
+    return [w.reshape(ng, -1, w.shape[-1]) for w in result[:n]], result[n:]
+
+
+def mix_back_kernel(grid, dims, shapes, *refs):
+    n = len(shapes)
+    terms, refs = refs[:n], refs[n:]
+    gact, x_in, mixed, carry, par, alive, spans, tok, pre, direct, small_in, *refs = refs
+    sums, refs = refs[:n], refs[n:]
+    (gtok_out, small_out,
+     g_rows, gin_rows, before, bound, m_all, k_all, small, seq_in, seg_in,
+     sends_b, recv_b, s_send, s_recv, own_sem, send, recv, *scratch) = refs
     nq = grid.nq
     rows, width = gact.shape
     blocks = width // 128
-    s, g = lax.axis_index("seq"), lax.axis_index("seg")
-    seq_peer = [{"seq": lax.rem(s + d, nq), "seg": g} for d in range(1, nq)]
-    barrier = pltpu.get_barrier_semaphore()
-    for place in seq_peer:
-        pl.semaphore_signal(barrier, inc=1, device_id=place, device_id_type=MESH)
-    pl.semaphore_wait(barrier, nq - 1)
+    s = lax.axis_index("seq")
+    seq_peer, seg_peer = small_peers(grid)
+    meet(seq_peer + seg_peer)
+    steps = scatter_steps(grid, shapes, terms, sums, scratch, own_sem, Sems(send, recv))
+    little = SmallSum(grid, small, small_out, seq_in, seg_in, s_send, s_recv)
+
+    def pump(count=1):
+        for _ in range(count):
+            next(steps, None)
+
+    pump()
     for b in range(blocks):
         g_rows[pl.ds(b, rows, stride=blocks), :] = gact[:, b * 128 : b * 128 + 128].astype(jnp.float32)
 
@@ -618,6 +763,7 @@
             bound.at[s], bound.at[s], sends_b.at[d - 1], recv_b.at[d - 1],
             device_id=seq_peer[d - 1], device_id_type=MESH))
         out[-1].start()
+    pump()
     for d in range(1, nq):
         came = bound.at[lax.rem(s + nq - d, nq)]
         pltpu.make_async_remote_copy(
@@ -643,6 +789,8 @@
             return tuple(keep[j] * (state[t] * a) + x for t, j in enumerate(js))
 
         lax.fori_loop(0, rows, ahead, tuple(carry[j] for j in js), unroll=4)
+        if j0:
+            pump()
 
         def back(i, held):
             flow, m_sum, k_sum, om_sum = held
@@ -668,44 +816,93 @@
             0, rows, back, (tuple(flow_in[j] for j in js), zeros, zeros, zero), unroll=4
         )
         for t, j in enumerate(js):
-            m_out[j] = m_sum[t]
-            k_out[j] = k_sum[t]
+            m_all[j] = m_sum[t]
+            k_all[j] = k_sum[t]
         if j0 == 0:
-            om_out[...] = om_sum
-    for b in range(blocks):
-        gin_out[:, b * 128 : b * 128 + 128] = gin_rows[pl.ds(b, rows, stride=blocks), :].astype(jnp.bfloat16)
+            m_all[dims] = om_sum
+        pump()
+
+    gain = [par[4 * dims, b : b + 1, :] for b in range(blocks)]
+    lanes = [slice(b * 128, b * 128 + 128) for b in range(blocks)]
+    step_rows = 32
+
+    def norm_back(i, gains):
+        at = pl.ds(pl.multiple_of(i * step_rows, step_rows), step_rows)
+        v = tok[at, :].astype(jnp.float32)
+        r = lax.rsqrt(jnp.mean(v * v, axis=1, keepdims=True) + epsilon)
+        gy = []
+        for b in range(blocks):
+            came = gin_rows[pl.ds(i * step_rows * blocks + b, step_rows, stride=blocks), :]
+            gy.append(pre[at, lanes[b]] + came.astype(jnp.bfloat16).astype(jnp.float32))
+        scaled = [gy[b] * gain[b] for b in range(blocks)]
+        dots = sum(jnp.sum(scaled[b] * v[:, lanes[b]], axis=1, keepdims=True) for b in range(blocks))
+        pull = r * r * (dots / width)
+        new = []
+        for b in range(blocks):
+            vb = v[:, lanes[b]]
+            gx = r * (scaled[b] - vb * pull)
+            gtok_out[at, lanes[b]] = (direct[at, lanes[b]] + gx).astype(jnp.bfloat16)
+            new.append(gains[b] + jnp.sum(gy[b] * (vb * r), axis=0, keepdims=True))
+        return tuple(new)
+
+    gains = lax.fori_loop(
+        0, rows // step_rows, norm_back, tuple(jnp.zeros((1, 128), jnp.float32) for _ in range(blocks))
+    )
+    for e in range(nq):
+        b = block_of(e, nq, blocks)
+        small[e] = small_in[e]
+        small[e, 0:dims] = m_all[0:dims, b, :]
+        small[e, dims : 2 * dims] = k_all[:, b, :]
+        small[e, 2 * dims : 2 * dims + 1] = m_all[dims, b : b + 1, :]
+        small[e, 2 * dims + 1 : 2 * dims + 2] = gains[b]
+    little.start()
+    pump()
+    little.middle()
     for copy in out:
         copy.wait_send()
-
-
-def mix_backward(grid, gact, x_in, mixed, carry, par, alive, spans, collective_id):
+    for _ in steps:
+        pass
+    little.end()
+
+
+def mix_backward(grid, terms, cuts, gact, x_in, mixed, carry, par, alive, spans, tok, pre, direct, small, collective_id):
     rows, width = gact.shape
-    nq = grid.nq
+    nq, ng = grid.nq, grid.ng
     blocks, dims, few = width // 128, carry.shape[0], 4
     f = jnp.float32
     vm = pl.BlockSpec(memory_space=pltpu.VMEM)
-    return pl.pallas_call(
-        functools.partial(mix_back_kernel, grid, dims),
-        out_shape=[
-            jax.ShapeDtypeStruct((rows, width), jnp.bfloat16),
-            jax.ShapeDtypeStruct((dims, blocks, 128), f),
-            jax.ShapeDtypeStruct((dims, blocks, 128), f),
-            jax.ShapeDtypeStruct((blocks, 128), f),
-        ],
-        in_specs=[vm] * 7,
-        out_specs=[vm] * 4,
+    shapes, parts, outs, scratch, count = scatter_plan(grid, terms, cuts)
+    n = len(parts)
+    result = pl.pallas_call(
+        functools.partial(mix_back_kernel, grid, dims, shapes),
+        out_shape=outs
+        + [jax.ShapeDtypeStruct((rows, width), jnp.bfloat16), jax.ShapeDtypeStruct(small.shape[1:], f)],
+        in_specs=[ANY] * n + [vm] * 11,
+        out_specs=[vm] * (n + 2),
         scratch_shapes=[
             pltpu.VMEM((rows * blocks, 128), f),
             pltpu.VMEM((rows * blocks, 128), f),
             pltpu.VMEM((rows, few, blocks, 128), f),
             pltpu.VMEM((nq, dims, blocks, 128), f),
+            pltpu.VMEM((dims + 1, blocks, 128), f),
+            pltpu.VMEM((dims, blocks, 128), f),
+            pltpu.VMEM(small.shape, f),
+            pltpu.VMEM((nq - 1,) + small.shape[1:], f),
+            pltpu.VMEM((ng - 1,) + small.shape[1:], f),
             pltpu.SemaphoreType.DMA((nq - 1,)),
             pltpu.SemaphoreType.DMA((nq - 1,)),
-        ],
+            pltpu.SemaphoreType.DMA((nq + ng - 2,)),
+            pltpu.SemaphoreType.DMA((nq + ng - 2,)),
+            pltpu.SemaphoreType.DMA((n, 2)),
+            pltpu.SemaphoreType.DMA((count,)),
+            pltpu.SemaphoreType.DMA((count,)),
+        ]
+        + scratch,
         compiler_params=pltpu.CompilerParams(
-            collective_id=collective_id, has_side_effects=True, vmem_limit_bytes=40 << 20
+            collective_id=collective_id, has_side_effects=True, vmem_limit_bytes=62 << 20
         ),
-    )(gact, x_in, mixed, carry, par, alive, spans)
+    )(*parts, gact, x_in, mixed, carry, par, alive, spans, tok, pre, direct, small)
+    return [v.reshape(-1, t.shape[-1]) for v, t in zip(result, terms)], result[n], result[n + 1]
 
 
 def rms_forward(values, gain):
@@ -807,55 +1004,37 @@
     alive = jnp.broadcast_to(alive[:, None], (row_count, 128))
 
     tokens_flat = tokens.reshape(token_count, model_width).astype(jnp.float32)
-    normed_b, active, x_rows, mixed_rows, carry, par, affine = mix_forward(
-        grid, tokens.reshape(token_count, model_width), tile, alive, spans, dims, 0
-    )
-    mix_full, value_full, out_full, ffn_in_full, ffn_out_full = gather_all(
-        grid, [mix_weight, value_weight, out_weight, ffn_in, ffn_out], [4, 2, 2, 4, 4], 1
-    )
-    gain_one = par[4 * dims].reshape(-1)
-    gain_two = par[4 * dims + 2].reshape(-1)
-    inverse_one = lax.rsqrt(jnp.mean(tokens_flat * tokens_flat, axis=-1, keepdims=True) + epsilon)
-
-    projected = times(active, mix_full)
-    update = jax.nn.sigmoid(projected[:, :model_width])
-    gate_pre = projected[:, model_width : model_width + zdim + vdim]
-    gate_rows = jax.nn.silu(gate_pre)
-    shared = gate_rows[:, :zdim]
-    reset_gate = gate_rows[:, zdim:]
-    candidate = projected[:, model_width + zdim + vdim :]
-    value_pre = times(normed_b, value_full)
-    values_b = jax.nn.silu(value_pre).astype(jnp.bfloat16)
-    scale_q = zdim ** (-0.5)
-    query_b = (scale_q * (shared * affine[0] + affine[1])).astype(jnp.bfloat16)
-    key_b = (shared * affine[2] + affine[3]).astype(jnp.bfloat16)
     positions_rows = seq_index * row_count + jnp.arange(row_count, dtype=jnp.int32)
     docs_rows = jnp.sum((starts[:, None, :] <= positions_rows[None, :, None]).astype(jnp.int32), axis=2)
     block_count = token_count // STRETCH
     block_docs = docs_rows.reshape(block_count, STRETCH)
     offsets = jnp.arange(STRETCH)
     allowed = (block_docs[:, :, None] == block_docs[:, None, :]) & (offsets[:, None] >= offsets[None, :])[None]
+    mask = allowed.astype(jnp.float32).reshape(token_count, STRETCH)
+    tokens_low = tokens.reshape(token_count, model_width)
+    weights, forward = mix_forward(
+        grid, [mix_weight, value_weight, out_weight, ffn_in, ffn_out], GATHER_CUTS, tokens_low, tile, alive, spans, mask, dims, 0
+    )
+    mix_full, value_full, out_full, ffn_in_full, ffn_out_full = weights
+    (normed_b, active, x_rows, mixed_rows, carry, par, affine, probs, out_one, normed_two_b, result,
+     projected, value_pre, attended, hidden_in, hidden_pre, ffn_hidden, ffn_act) = forward
+    gain_two = par[4 * dims + 2].reshape(-1)
+    update = jax.nn.sigmoid(projected[:, :model_width])
+    gate_pre = projected[:, model_width : model_width + zdim + vdim]
+    gate_rows = jax.nn.silu(gate_pre)
+    shared = gate_rows[:, :zdim]
+    reset_gate = gate_rows[:, zdim:]
+    values_b = jax.nn.silu(value_pre).astype(jnp.bfloat16)
+    scale_q = zdim ** (-0.5)
+    query_b = (scale_q * (shared * affine[0] + affine[1])).astype(jnp.bfloat16)
+    key_b = (shared * affine[2] + affine[3]).astype(jnp.bfloat16)
     query_blk = query_b.reshape(block_count, STRETCH, zdim)
     key_blk = key_b.reshape(block_count, STRETCH, zdim)
     value_blk = values_b.reshape(block_count, STRETCH, vdim)
-    scores = masked_scores(query_blk, key_blk, allowed)
-    row_top = jnp.max(scores, axis=2, keepdims=True)
-    expo_scores = jnp.exp(scores - row_top)
-    row_total = jnp.sum(expo_scores, axis=2, keepdims=True)
-    probs = expo_scores / row_total
+    probs = probs.reshape(block_count, STRETCH, STRETCH)
     probs_b = probs.astype(jnp.bfloat16)
-    attended = jnp.einsum("cij,cjv->civ", probs_b, value_blk, preferred_element_type=jnp.float32).reshape(
-        token_count, vdim
-    )
-    hidden_in = (attended * reset_gate).astype(jnp.bfloat16)
-    hidden_pre = candidate + times(hidden_in, out_full)
     hidden_act = jax.nn.silu(hidden_pre)
-    out_one = tokens_flat + update * (hidden_act - tokens_flat)
-    normed_two, inverse_two = rms_forward(out_one, gain_two)
-    normed_two_b = normed_two.astype(jnp.bfloat16)
-    ffn_hidden = times(normed_two_b, ffn_in_full)
-    ffn_act = jax.nn.silu(ffn_hidden).astype(jnp.bfloat16)
-    result = (out_one + times(ffn_act, ffn_out_full)).astype(jnp.bfloat16)
+    inverse_two = lax.rsqrt(jnp.mean(out_one * out_one, axis=-1, keepdims=True) + epsilon)
 
     grad_y_b = cotangent.reshape(token_count, model_width)
     grad_ffn_out = over_rows(ffn_act, grad_y_b, ng)
@@ -902,25 +1081,20 @@
     )
     grad_mix = over_rows(active, grad_proj_b, ng)
     grad_active_b = against(grad_proj_b, mix_full).astype(jnp.bfloat16)
-    grad_ema_in, m_part, k_part, omega_part = mix_backward(
-        grid, grad_active_b, x_rows, mixed_rows, carry, par, alive, spans, 2
-    )
     grad_vpre_b = (grad_values * silu_slope(value_pre)).astype(jnp.bfloat16)
     grad_value = over_rows(normed_b, grad_vpre_b, ng)
-    grad_normed = against(grad_vpre_b, value_full) + grad_ema_in.astype(jnp.float32)
-    grad_norm_one, grad_gain_one = rms_backward(grad_normed, tokens_flat, inverse_one, gain_one)
-    grad_tokens = (grad_tokens_flat + grad_norm_one).astype(jnp.bfloat16)
+    grad_normed = against(grad_vpre_b, value_full)
 
     small = jnp.concatenate(
-        [m_part, k_part, omega_part[None], grad_gain_one.reshape(1, blocks, 128), grad_gain_two.reshape(1, blocks, 128)],
-        axis=0,
-    ).transpose(1, 0, 2)
+        [jnp.zeros((blocks, 2 * dims + 2, 128), jnp.float32), grad_gain_two.reshape(blocks, 1, 128)], axis=1
+    )
     if nq != blocks:
         small = jnp.take(small, np.arange(nq) * blocks // nq, axis=0)
     small = jnp.concatenate([small, jnp.broadcast_to(grad_affine[None], (nq, 4, 128))], axis=1)
     small = jnp.pad(small, ((0, 0), (0, -small.shape[1] % 8), (0, 0)))
-    sums, (g_mix, g_value, g_out, g_ffn_in, g_ffn_out) = scatter_all(
-        grid, small, [grad_mix, grad_value, grad_out_weight, grad_ffn_in, grad_ffn_out], [4, 2, 2, 4, 4], 3, 60 << 20
+    (g_ffn_out, g_ffn_in, g_out, g_mix, g_value), grad_tokens, sums = mix_backward(
+        grid, [grad_ffn_out, grad_ffn_in, grad_out_weight, grad_mix, grad_value], SCATTER_CUTS, grad_active_b, x_rows,
+        mixed_rows, carry, par, alive, spans, tokens_low, grad_normed, grad_tokens_flat, small, 1
     )
     return (
         result.reshape(seg_count, row_count, model_width),

time: 598 us -> 516 us (0.86)
  matrix products: 79.2 us -> 39.3 us
  local copies, waits for them, and re-layouts: 63.6 us -> 37.8 us
  other arithmetic: 43.3 us -> 32.7 us
    dot_general x22 -> x0, matrix products: 28.1 us -> none  [the longest x20 24.7 us: times(): jnp.dot(left, pieces[i], preferred_element_type=jnp.float32)]
    unnamed x162 -> x90, local copies, waits for them, and re-layouts: 30.3 us -> 14.2 us
    reshape x6 -> x1, local copies, waits for them, and re-layouts: 8.04 us -> 1 us  [body(): probs = probs.reshape(block_count, STRETCH, STRETCH)]
    dot_general x20, matrix products: 30.8 us -> 24.1 us  [against(): lax.dot_general(left[:, i * n:i * n + n], pieces[i], (((1,), (1,)), ((),...]
    pallas_call x4 -> x2, Pallas kernels: 398 us -> 396 us  [the longest x1 221 us: mix_forward(): pl.pallas_call(functools.partial(mix_kernel, grid, width, dims, shapes),...]
where the time goes in v2:
time: 516 us; the launch traced here: 507 us
  Pallas kernels  396 us (77%)
  matrix products  39.3 us (8%)
  local copies, waits for them, and re-layouts  37.8 us (7%)
  other arithmetic  32.7 us (6%)
    pallas_call x1, Pallas kernels, mix_forward(): pl.pallas_call(functools.partial(mix_kernel, grid, width, dims, shapes),...  221 us
    pallas_call x1, Pallas kernels, mix_backward(): pl.pallas_call(functools.partial(mix_back_kernel, grid, dims, shapes), ou...  175 us
    dot_general x20, matrix products, against(): lax.dot_general(left[:, i * n:i * n + n], pieces[i], (((1,), (1,)), ((),...  24.1 us
    another operation x5, other arithmetic, over_rows(): jnp.stack([lax.dot_general(left, right[:, i * n:i * n + n], (((0,), (0,))...  16.7 us
    unnamed x90, local copies, waits for them, and re-layouts  14.2 us
    dot_general x20, matrix products, over_rows(): lax.dot_general(left, right[:, i * n:i * n + n], (((0,), (0,)), ((), ()))...  13.8 us
    another operation x1, local copies, waits for them, and re-layouts, over_rows(): jnp.stack([lax.dot_general(left, right[:, i * n:i * n + n], (((0,), (0,))...  11.8 us

profile of v2, /device:TPU:0, one launch (start us, length us, event | category | flops | bytes accessed | tf_op | source)
XLA Modules:
  0.0 507.3 jit_solution(3080820982186389159)
XLA Ops:
  0.7 3.5 concatenate.16
  4.2 0.7 dynamic_update_slice.6
  5.7 0.8 fusion.85
  6.5 0.8 broadcast_in_dim.54.refs_7_.refs_10_
  7.3 0.7 convert_reduce_fusion
  8.0 0.8 fusion.66.refs_9_
  9.6 1.8 copy.61
  11.4 220.5 %shard_map.271 = (bf16[2,2,4,2,8,16,1056]{6,5,4,3,2,1,0:T(8,128)(2,1)}, bf16[2,2,4,2,8,16,512]{6,5,4,3,2,1,0:T(8,128)(2,1)}, bf16[2,2,4,2,8,32,256]{6,5,4,3,2,1,...) custom-call(bf16[8,16,1056]{2,1,0:T(8,128)(2,1)} %bitcast.298, ...), custom_call_target="tpu_custom_call" | custom-call | tf_op jit(solution)/shard_map/pallas_call | solution.py:684
  232.0 2.4 fusion.20
  234.4 0.8 slice_bitcast_fusion.58
  235.3 2.5 fusion.26
  238.1 0.8 convolution_add_fusion.2
  238.9 0.7 convolution_add_fusion.1
  239.7 1.4 copy-done.30
  241.1 2.2 fusion.2
  243.8 0.7 fusion.24
  244.5 0.7 fusion.23
  245.3 0.7 fusion.22
  246.0 0.7 slice_bitcast_fusion.54
  246.9 1.1 multiply_reduce_fusion
  248.1 2.9 subtract_multiply_fusion
  251.0 3.0 multiply_convert_fusion.1
  255.5 1.1 copy-done.15
  256.5 2.0 fusion.21
  258.5 1.0 copy.67
  259.9 1.2 copy-done.14
  261.1 0.9 fusion.27
  263.0 1.2 broadcast_multiply_fusion.1
  264.4 0.7 pad.4.refs_15_
  266.6 1.5 convolution_add_fusion.6.refs_13_
  268.4 0.8 fusion.19
  269.2 2.7 fusion.17
  272.0 2.6 fusion.16
  274.7 1.1 fusion.15
  275.9 1.7 fusion.38.refs_5_
  279.5 2.4 pad_maximum_fusion.4
  281.9 0.8 fusion.7
  282.7 1.0 fusion.8
  283.7 1.0 fusion.9
  284.8 1.1 fusion.10
  285.9 4.0 pad_maximum_fusion
  289.9 11.8 %copy.69 = bf16[4,1024,1056]{2,1,0:T(8,128)(2,1)} copy(bf16[4,1024,1056]{1,2,0:T(8,128)(2,1)} %pad_maximum_fusion) | data formatting | bytes 17301504 | tf_op jit(solution)/shard_map/stack | solution.py:943
  303.7 2.3 pad_maximum_fusion.3
  306.7 0.7 convert_bitcast_fusion.3
  307.4 0.7 convert_bitcast_fusion.2
  308.1 0.7 convert_bitcast_fusion.1
  308.9 0.7 convert_bitcast_fusion
  309.7 4.1 pad_maximum_fusion.2
  313.8 0.8 fusion.3
  314.6 0.8 fusion.4
  315.4 0.8 fusion.5
  316.1 0.8 fusion.6
  316.9 4.0 pad_maximum_fusion.1
  320.9 175.0 %shard_map.272 = (f32[8,64,256]{2,1,0:T(8,128)}, f32[8,16,1024]{2,1,0:T(8,128)}, f32[4,64,256]{2,1,0:T(8,128)}, f32[8,16,1056]{2,1,0:T(8,128)}, f32[4,32,512]{2,...) custom-call(bf16[2,2,4,2,8,64,256]{6,5,4,3,2,1,0:T(8,128)(2,1)} %bitcast.266, ...), custom_call_target="tpu_custom_call" | custom-call | tf_op jit(solution)/shard_map/pallas_call | solution.py:876
  495.9 2.2 copy.71
  498.1 1.3 dynamic-slice_bitcast_fusion.5
  499.5 1.4 subtract_multiply_fusion.1
  500.9 1.4 dynamic-slice_bitcast_fusion.2
  502.3 0.8 copy.85
  503.0 0.8 copy.86
  503.8 0.7 copy.87
  504.6 0.7 copy.88
  505.3 0.8 copy.89
  506.1 0.8 copy.90
  (123 shorter events, 12.1 us)
Async XLA Ops:
  5.7 5.8 %copy-start.25 = (f32[72,128]{1,0:T(8,128)}, f32[72,128]{1,0:T(8,128)S(1)}, u32[]{:S(2)}) copy-start(f32[72,128]{1,0:T(8,128)S(1)} %dynamic_update_slice.7.refs_6_) | copy-start | bytes 110596
  232.0 3.3 copy-start.16
  232.0 5.8 %slice-start.2 = ((s8[8388608]{0:T(1024)(128)(4,1)}), s8[4194304]{0:T(1024)(128)(4,1)S(1)}, s32[]{:S(2)}) async-start(s8[8388608]{0:T(1024)(128)(4,1)} %bitcast.274), calls=%async_computation.2 | async-start | bytes 8388608
  235.2 2.8 slice-start.3
  238.9 2.2 copy-start.30
  238.9 4.4 slice-start.7
  241.1 2.7 slice-start.8
  243.3 3.6 copy-start.12
  245.3 1.5 copy-start.2
  248.0 2.9 copy-start.8
  248.1 2.9 copy-start.18
  251.0 3.0 copy-start.11
  254.0 1.5 copy-start.6
  254.9 1.6 copy-start.15
  259.5 1.6 copy-start.14
  262.0 3.1 copy-start.10
  262.6 5.4 %slice-start = ((s8[4325376]{0:T(1024)(128)(4,1)}), s8[4194304]{0:T(1024)(128)(4,1)S(1)}, s32[]{:S(2)}) async-start(s8[4325376]{0:T(1024)(128)(4,1)} %bitcast.269), calls=%async_computation | async-start | bytes 8388608
  265.6 2.5 slice-start.1
  265.6 9.0 %slice-start.4 = ((s8[9437184]{0:T(1024)(128)(4,1)}), s8[1048576]{0:T(1024)(128)(4,1)S(1)}, s32[]{:S(2)}) async-start(s8[9437184]{0:T(1024)(128)(4,1)} %bitcast.302), calls=%async_computation.4 | async-start | bytes 2097152
  266.5 1.9 copy-start.4
  266.6 8.1 %slice-start.5 = ((s8[9437184]{0:T(1024)(128)(4,1)}), s8[4194304]{0:T(1024)(128)(4,1)S(1)}, s32[]{:S(2)}) async-start(s8[9437184]{0:T(1024)(128)(4,1)} %bitcast.302), calls=%async_computation.5 | async-start | bytes 8388608
  269.2 5.4 %slice-start.6 = ((s8[9437184]{0:T(1024)(128)(4,1)}), s8[4194304]{0:T(1024)(128)(4,1)S(1)}, s32[]{:S(2)}) async-start(s8[9437184]{0:T(1024)(128)(4,1)} %bitcast.302), calls=%async_computation.6 | async-start | bytes 8388608
  272.0 2.7 copy-start.7
  274.7 1.2 copy-start.9
  275.8 1.7 copy-start.3
  279.5 2.4 copy-start.1
  289.9 11.9 %copy-start = (bf16[256,2048]{1,0:T(8,128)(2,1)S(1)}, bf16[256,2048]{1,0:T(8,128)(2,1)}, u32[]{:S(2)}) copy-start(bf16[256,2048]{1,0:T(8,128)(2,1)} %get-tuple-element.50) | copy-start | bytes 3145732
  303.7 2.3 copy-start.5
  303.7 2.9 copy-start.13
  309.6 4.1 copy-start.17
  309.7 4.1 copy-start.31
  320.9 178.6 %copy-start.26 = (bf16[32,16]{0,1:T(8,128)(2,1)S(1)}, bf16[32,16]{0,1:T(8,128)(2,1)}, u32[]{:S(2)}) copy-start(bf16[32,16]{0,1:T(8,128)(2,1)} %param.19) | copy-start | bytes 3076
  320.9 178.6 %copy-start.27 = (bf16[32,16]{0,1:T(8,128)(2,1)S(1)}, bf16[32,16]{0,1:T(8,128)(2,1)}, u32[]{:S(2)}) copy-start(bf16[32,16]{0,1:T(8,128)(2,1)} %param.20) | copy-start | bytes 3076
  320.9 178.6 %copy-start.28 = (bf16[32,16]{0,1:T(8,128)(2,1)S(1)}, bf16[32,16]{0,1:T(8,128)(2,1)}, u32[]{:S(2)}) copy-start(bf16[32,16]{0,1:T(8,128)(2,1)} %param.21) | copy-start | bytes 3076
  320.9 178.6 %copy-start.29 = (bf16[32,16]{0,1:T(8,128)(2,1)S(1)}, bf16[32,16]{0,1:T(8,128)(2,1)}, u32[]{:S(2)}) copy-start(bf16[32,16]{0,1:T(8,128)(2,1)} %param.22) | copy-start | bytes 3076
  320.9 181.4 %copy-start.19 = (bf16[256,1024]{1,0:T(8,128)(2,1)S(1)}, bf16[256,1024]{1,0:T(8,128)(2,1)}, u32[]{:S(2)}) copy-start(bf16[256,1024]{1,0:T(8,128)(2,1)} %get-tuple-element.45) | copy-start | bytes 1572868
  495.9 7.2 %copy-start.22 = (bf16[256,1024]{1,0:T(8,128)(2,1)S(1)}, bf16[256,1024]{1,0:T(8,128)(2,1)}, u32[]{:S(2)}) copy-start(bf16[256,1024]{1,0:T(8,128)(2,1)} %get-tuple-element.68) | copy-start | bytes 1572868
  495.9 7.9 %copy-start.24 = (f32[4,32,512]{2,1,0:T(8,128)S(1)}, f32[4,32,512]{2,1,0:T(8,128)}, u32[]{:S(2)}) copy-start(f32[4,32,512]{2,1,0:T(8,128)} %get-tuple-element.71) | copy-start | bytes 786436
  495.9 8.6 %copy-start.23 = (f32[4,64,256]{2,1,0:T(8,128)S(1)}, f32[4,64,256]{2,1,0:T(8,128)}, u32[]{:S(2)}) copy-start(f32[4,64,256]{2,1,0:T(8,128)} %get-tuple-element.72) | copy-start | bytes 786436
  495.9 9.3 %copy-start.21 = (f32[8,16,1024]{2,1,0:T(8,128)S(1)}, f32[8,16,1024]{2,1,0:T(8,128)}, u32[]{:S(2)}) copy-start(f32[8,16,1024]{2,1,0:T(8,128)} %get-tuple-element.73) | copy-start | bytes 1572868
  498.1 7.9 %copy-start.20 = (f32[8,64,256]{2,1,0:T(8,128)S(1)}, f32[8,64,256]{2,1,0:T(8,128)}, u32[]{:S(2)}) copy-start(f32[8,64,256]{2,1,0:T(8,128)} %get-tuple-element.74) | copy-start | bytes 1572868
